TPU v7x, 32 devices: a whole 2x2x4 slice. The times are simulated.
32 devices in a mesh: grp: 2 (over x), tmpl: 8 (over z, y), tm: 2 (over core).
Axes of the slice: x: 2, y: 2, z: 4, core: 2. Of those that a mesh axis runs over, the one named last changes fastest.
Arguments:
- spectra: bfloat16 [1024, 4, 8192], P(('grp', 'tm', 'tmpl')), parts along dimension 0, may hold values from -6 to 6
- offsets: int32 [1024, 16], P(('grp', 'tm'), 'tmpl'), parts along dimension 0, may hold values from 0 to 1008
- fractions: float32 [4096], P(('grp', 'tmpl')), parts along dimension 0, may hold values from 0.1 to 0.9
- antenna: float32 [1024, 4], P('grp'), parts along dimension 0, may hold values from -2 to 2, as said below
- starts: int32 [64], P('grp'), parts along dimension 0, may hold values from 0 to 255
- durations: int32 [64], P('grp'), parts along dimension 0, may hold values from 48 to 256
Outputs:
- fstat_map: float32 [32, 32, 4096], P('tm', None, ('grp', 'tmpl')), parts along dimension 2
- loudest: float32 [64, 32], P(('grp', 'tm')), parts along dimension 0
There are 2 independent parts, one for each index of `grp`. A program takes and returns all parts, laid end to end along the dimension named above; each array names one. Nothing has to cross between parts.
Inputs may be any that keep to these rules, and one draw needn't show every extreme that they name: `antenna`: each detector's responses a and b turn once every 48 SFTs with magnitudes that vary from SFT to SFT.
All inputs are finite; a program needn't handle non-finite values.
Results may differ from a plain program's by a relative error of at most 0.0051.
Values may be sent and summed in bfloat16 or wider, within the bound.
No kernel may reach another device: no remote copies, remote signals or barrier semaphores. Data moves between devices by JAX's collectives and lax.ppermute only.
A program may use at most 128 MiB of HBM per device.

v0:
```python
import functools

import jax
import jax.numpy as jnp
from jax import lax
from jax.experimental import pallas as pl
from jax.experimental.pallas import tpu as pltpu
from jax.sharding import PartitionSpec as P

W = 16
LANES = 128
NT = (((1,), (1,)), ((), ()))


def iota(shape, axis):
    return lax.broadcasted_iota(jnp.int32, shape, axis)


def order(size, first):
    members = list(range(size))
    members[0], members[first] = first, 0
    return members


def hold_kernel(spec_ref, out_ref, sem):
    copy = pltpu.make_async_copy(spec_ref, out_ref, sem)
    copy.start()
    copy.wait()


def hold(spectra):
    return pl.pallas_call(
        hold_kernel,
        out_shape=jax.ShapeDtypeStruct(spectra.shape, spectra.dtype),
        in_specs=[pl.BlockSpec(memory_space=pl.ANY)],
        out_specs=pl.BlockSpec(memory_space=pltpu.VMEM),
        scratch_shapes=[pltpu.SemaphoreType.DMA],
        compiler_params=pltpu.CompilerParams(vmem_limit_bytes=8 * 1024 * 1024),
        cost_estimate=pl.CostEstimate(flops=0, bytes_accessed=4 * spectra.size, transcendentals=0),
        name="hold",
    )(spectra)


def pick_kernel(bands_in, bands_out, me_ref, offset_ref, spec_ref, out_ref, place_ref, turn_ref):
    rows, _, bins = spec_ref.shape
    bands, blocks, _ = offset_ref.shape
    band_width = bins // bands
    groups = rows // 8
    chunks = band_width // LANES
    width = blocks * W
    first = me_ref[0] * rows
    columns = pl.ds(pl.multiple_of(first // LANES * LANES, LANES), LANES)
    offsets = jnp.concatenate([offset_ref[bands_in.index(band), :, columns] for band in range(bands)], axis=0).astype(jnp.float32)
    lane = iota(offsets.shape, 1)
    offsets = jnp.take_along_axis(offsets, (lane >> 2) + first & (LANES - 1), axis=1, mode="promise_in_bounds")
    offsets = jnp.concatenate([offsets, jnp.zeros((LANES - bands * blocks, LANES), jnp.float32)], axis=0)
    upright = jnp.transpose(offsets).astype(jnp.int32)
    lane = iota((32, LANES), 1)
    places = upright[0:32]
    for group in range(1, groups):
        turned = pltpu.roll(upright[group * 32 : group * 32 + 32], group * bands * blocks, 1)
        places = jnp.where(lane < group * bands * blocks, places, turned)
    lane = iota((8, LANES), 1)
    lane_group = lane // width
    source = lane_group * (bands * blocks) + lane // W % blocks
    for band in range(bands):
        for pair in range(4):
            place = jnp.take_along_axis(places[pair * 8 : pair * 8 + 8], source + band * blocks, axis=1, mode="promise_in_bounds")
            place_ref[band, pair] = place + ((lane & (W - 1)) + lane_group * band_width)

    def step(band, carry):
        for pair in range(4):
            place = place_ref[band, pair]
            lane_id = place & (LANES - 1)
            chosen = place >> 7
            tile = jnp.zeros((8, LANES), jnp.float32)
            for group in range(groups):
                for chunk in range(chunks):
                    start = pl.multiple_of(band * band_width + chunk * LANES, LANES)
                    values = spec_ref[pl.ds(group * 8 + pair * 2, 2), :, pl.ds(start, LANES)]
                    values = values.astype(jnp.float32).reshape(8, LANES)
                    moved = jnp.take_along_axis(values, lane_id, axis=1, mode="promise_in_bounds")
                    tile = jnp.where(chosen == group * chunks + chunk, moved, tile)
            turn_ref[band, pl.ds(pair * 8, 8), :] = tile
        return carry

    lax.fori_loop(0, bands, step, 0, unroll=2)
    tiles = {}
    for band in range(bands):
        parts = [turn_ref[band, pl.ds(part, 8, stride=4), :] for part in range(4)]
        for group in range(groups):
            tile = jnp.zeros((8, LANES), jnp.float32)
            for part in range(4):
                amount = (part - group) * width % LANES
                turned = pltpu.roll(parts[part], amount, 1) if amount else parts[part]
                tile = jnp.where(lane_group == part, turned, tile)
            tiles[band, group] = tile
    wanted = [tiles[band, group] for band in bands_out for group in range(groups)]
    for n in range(0, len(wanted), 2):
        out_ref[n * 8 : n * 8 + 16, :] = jnp.concatenate(wanted[n : n + 2], axis=0).astype(jnp.bfloat16)


def pick(me, offsets, spectra, bands_in, bands_out):
    rows, bands = spectra.shape[0], offsets.shape[0]
    out_rows = len(bands_out) * rows
    vmem = pl.BlockSpec(memory_space=pltpu.VMEM)
    return pl.pallas_call(
        functools.partial(pick_kernel, bands_in, bands_out),
        out_shape=jax.ShapeDtypeStruct((out_rows, LANES), jnp.bfloat16),
        in_specs=[pl.BlockSpec(memory_space=pltpu.SMEM), vmem, vmem],
        out_specs=vmem,
        scratch_shapes=[
            pltpu.VMEM((bands, 4, 8, LANES), jnp.int32),
            pltpu.VMEM((bands, 32, LANES), jnp.float32),
        ],
        compiler_params=pltpu.CompilerParams(vmem_limit_bytes=8 * 1024 * 1024),
        cost_estimate=pl.CostEstimate(flops=10_000_000, bytes_accessed=2 * spectra.size, transcendentals=0),
        name="pick",
    )(me, offsets, spectra)


def split(values, count):
    parts = []
    for _ in range(count):
        part = values.astype(jnp.bfloat16)
        parts.append(part)
        values = values - part.astype(jnp.float32)
    return parts


def prepare_kernel(first, run, durations_ref, starts_ref, antenna_ref, fractions_ref, mask_ref, weigh_ref, coef_ref, kernel_ref):
    rows = starts_ref.shape[0]
    count = durations_ref.shape[0]
    sfts = antenna_ref.shape[1]
    sft = iota((rows, sfts), 1)
    sft = jnp.where(sft // run == 0, sft + first * run, jnp.where(sft // run == first, sft - first * run, sft))
    start = starts_ref[:, 0:1]
    after = sft >= start
    for j in range(count):
        inside = after & (sft < start + durations_ref[j])
        mask_ref[pl.ds(j * rows, rows), :] = jnp.where(inside, 1.0, 0.0).astype(jnp.bfloat16)
    antenna = jnp.concatenate([antenna_ref[...], jnp.zeros((4, sfts), jnp.float32)], axis=0)
    place = iota(antenna.shape, 1) // run
    after = pltpu.roll(antenna, sfts - first * run, 1)
    before = pltpu.roll(antenna, first * run, 1)
    antenna = jnp.where(place == 0, after, jnp.where(place == first, before, antenna))
    a1, a2, b1, b2 = (antenna[n : n + 1] for n in range(4))
    terms = jnp.concatenate([a1 * a1 + a2 * a2, b1 * b1 + b2 * b2, a1 * b1 + a2 * b2, jnp.zeros((5, sfts), jnp.float32)], axis=0)
    weights = sum(lax.dot_general(mask_ref[...], part, NT, preferred_element_type=jnp.float32) for part in split(terms, 3))
    wa, wb, wc = (weights[:, n : n + 1] for n in range(3))
    shape = (rows * count, LANES)
    late = iota(shape, 1) >= LANES // 2
    coef_ref[0] = jnp.broadcast_to(1.0 / wa, shape)
    coef_ref[1] = jnp.broadcast_to(wa / (wa * wb - wc * wc), shape)
    coef_ref[2] = jnp.where(late, jnp.broadcast_to(wc / wa, shape), 0.0)
    upright = jnp.transpose(jnp.concatenate([antenna, jnp.zeros((LANES - 8, sfts), jnp.float32)], axis=0))
    shape = (sfts, LANES)
    late = iota(shape, 1) >= LANES // 2
    weigh_ref[0] = jnp.where(late, upright[:, 3:4], upright[:, 0:1])
    weigh_ref[1] = jnp.where(late, upright[:, 2:3], upright[:, 1:2])
    fractions = fractions_ref[...]
    templates = fractions.shape[1]
    blocks = kernel_ref.shape[1] // (4 * LANES)
    bin_id = iota((W, templates), 0)
    distance = fractions + (W // 2 - 1) - bin_id.astype(jnp.float32)
    alternate = 1.0 - 2.0 * (bin_id % 2).astype(jnp.float32)
    values = (alternate * jnp.sin(jnp.pi * fractions) / (jnp.pi * distance)).astype(jnp.bfloat16)
    kernel_ref[...] = jnp.zeros_like(kernel_ref)
    for part in range(2):
        for c in range(4):
            for b in range(blocks):
                row = ((part * 4 + c) * blocks + b) * W
                column = (c * blocks + b) * LANES
                kernel_ref[pl.ds(row, W), pl.ds(column, LANES)] = values[:, b * LANES : (b + 1) * LANES]


def prepare(durations, starts, antenna, fractions, first, run):
    count, rows, sfts = durations.shape[0], starts.shape[0], antenna.shape[0]
    columns = 4 * fractions.shape[0]
    features = 4 * W * (fractions.shape[0] // LANES)
    vmem = pl.BlockSpec(memory_space=pltpu.VMEM)
    return pl.pallas_call(
        functools.partial(prepare_kernel, first, run),
        out_shape=(
            jax.ShapeDtypeStruct((count * rows, sfts), jnp.bfloat16),
            jax.ShapeDtypeStruct((2, sfts, LANES), jnp.float32),
            jax.ShapeDtypeStruct((3, count * rows, LANES), jnp.float32),
            jax.ShapeDtypeStruct((2 * features, columns), jnp.bfloat16),
        ),
        in_specs=[pl.BlockSpec(memory_space=pltpu.SMEM), vmem, vmem, vmem],
        out_specs=(vmem,) * 4,
        compiler_params=pltpu.CompilerParams(vmem_limit_bytes=16 * 1024 * 1024),
        cost_estimate=pl.CostEstimate(flops=100_000_000, bytes_accessed=4_000_000, transcendentals=0),
        name="prepare",
    )(durations, jnp.broadcast_to(starts[:, None], (rows, LANES)), antenna.T, fractions[None, :])


def statistic_kernel(windows_ref, mask_ref, weigh_ref, coef_ref, kernel_ref, map_ref, loudest_ref, found_ref):
    values = windows_ref[...].astype(jnp.float32)
    half = LANES // 2
    weighted = (weigh_ref[0] * values + weigh_ref[1] * pltpu.roll(values, half, 1)).astype(jnp.bfloat16)
    sums = jnp.dot(mask_ref[...], weighted, preferred_element_type=jnp.float32)
    sums = sums - coef_ref[2] * pltpu.roll(sums, half, 1)
    parts = jnp.concatenate(split(sums, 2), axis=1)
    found_ref[...] = jnp.dot(parts, kernel_ref[...], preferred_element_type=jnp.float32)
    templates = map_ref.shape[1]
    rows = map_ref.shape[0] // loudest_ref.shape[1]
    copies = loudest_ref.shape[0]
    per_step = LANES // rows
    for step in range(map_ref.shape[0] // LANES):
        here = pl.ds(step * LANES, LANES)
        best = None
        for b in range(templates // LANES):
            ra, ia, rb, ib = (found_ref[here, pl.ds(c * templates + b * LANES, LANES)] for c in range(4))
            result = coef_ref[0, here, :] * (ra * ra + ia * ia) + coef_ref[1, here, :] * (rb * rb + ib * ib)
            map_ref[here, pl.ds(b * LANES, LANES)] = result
            best = result if best is None else jnp.maximum(best, result)
        best = jnp.max(jnp.transpose(best), axis=0, keepdims=True)
        for n in range(per_step):
            turned = best if n == 0 else pltpu.roll(best, LANES - n * rows, 1)
            for copy in range(copies):
                loudest_ref[copy, pl.ds(step * per_step + n, 1), :] = turned


def statistic(windows, mask, weigh, coef, kernel, rows, copies):
    count = mask.shape[0] // rows
    templates = kernel.shape[1] // 4
    vmem = pl.BlockSpec(memory_space=pltpu.VMEM)
    return pl.pallas_call(
        statistic_kernel,
        out_shape=(
            jax.ShapeDtypeStruct((count * rows, templates), jnp.float32),
            jax.ShapeDtypeStruct((copies, count, LANES), jnp.float32),
        ),
        in_specs=[vmem] * 5,
        out_specs=(vmem, vmem),
        scratch_shapes=[pltpu.VMEM((count * rows, 4 * templates), jnp.float32)],
        compiler_params=pltpu.CompilerParams(vmem_limit_bytes=16 * 1024 * 1024),
        cost_estimate=pl.CostEstimate(flops=400_000_000, bytes_accessed=4_000_000, transcendentals=0),
        name="statistic",
    )(windows, mask, weigh, coef, kernel)


def exchange(values, axis, members):
    return lax.all_to_all(values, axis, split_axis=0, concat_axis=0, axis_index_groups=[members], tiled=True)


def body(spectra, offsets, fractions, antenna, starts, durations):
    bands, cores = lax.axis_size("tmpl"), lax.axis_size("tm")
    sft_rows = spectra.shape[0]
    grid_size = starts.shape[0]
    my_rows = grid_size // cores
    me = lax.axis_index("tmpl").astype(jnp.int32)[None]
    by_band = order(bands, bands // 2)
    first = (cores - 1) * bands + bands // 2
    by_run = order(cores * bands, first)
    known = exchange(jnp.broadcast_to(offsets.T[None], (bands,) + offsets.T.shape), "tmpl", by_band)
    my_durations = lax.dynamic_slice_in_dim(durations, lax.axis_index("tm") * my_rows, my_rows, 0)
    prepared = prepare(my_durations, starts, antenna, fractions, first, sft_rows)
    me, prepared = lax.optimization_barrier((me, prepared))
    windows = pick(me, known, hold(spectra), by_band, [run % bands for run in by_run])
    arrived = exchange(windows.reshape(cores * bands, sft_rows, LANES), ("tm", "tmpl"), by_run)
    fstat_map, loudest = statistic(arrived.reshape(-1, LANES), *prepared, grid_size, bands)
    loudest = jnp.max(exchange(loudest, "tmpl", by_band)[:, :, :grid_size], axis=0)
    return (fstat_map.reshape(my_rows, grid_size, -1), loudest)


def solution(mesh):
    in_specs = (
        P(("grp", "tm", "tmpl"), None, None),
        P(("grp", "tm"), "tmpl"),
        P(("grp", "tmpl")),
        P("grp", None),
        P("grp"),
        P("grp"),
    )
    out_specs = (P("tm", None, ("grp", "tmpl")), P(("grp", "tm"), None))
    return jax.shard_map(body, mesh=mesh, in_specs=in_specs, out_specs=out_specs, check_vma=False)
```

profile of v0, /device:TPU:0, one launch (start us, length us, event | category | flops | bytes accessed | tf_op | source)
XLA Modules:
  0.0 38.5 jit_solution(12721652644157229207)
XLA Ops:
  0.6 1.3 %broadcast_in_dim.21 = s32[8,2,256]{2,1,0:T(2,128)} broadcast(s32[2,256]{1,0:T(2,128)} %bitcast.11), dimensions={1,2} | broadcast | bytes 18432 | tf_op jit(solution)/shard_map/broadcast_in_dim | solution.py:257
  1.9 7.8 %all-to-all-start = ((s32[8,2,256]{2,1,0:T(2,128)}), s32[8,2,256]{2,1,0:T(2,128)S(1)}, u32[]{:S(2)}, u32[]{:S(2)}) async-start(s32[8,2,256]{2,1,0:T(2,128)} %broadcast_in_dim.21), calls=%async_computation | async-start | bytes 32768 | tf_op jit(solution)/shard_map/all_to_all | solution.py:245
  9.8 0.0 copy-start
  9.8 1.6 %copy-done = bf16[32,4,8192]{2,1,0:T(4,128)(2,1)S(1)} copy-done((bf16[32,4,8192]{2,1,0:T(4,128)(2,1)S(1)}, bf16[32,4,8192]{2,1,0:T(4,128)(2,1)}, u32[]{:S(2)}) %copy-start) | copy-done | bytes 2097176
  11.4 0.0 copy-start.8
  11.4 0.2 hold.1.spec_ref
  11.5 0.5 %copy-done.8 = s32[32]{0:T(128)S(1)} copy-done((s32[32]{0:T(128)S(1)}, s32[32]{0:T(128)}, u32[]{:S(2)}) %copy-start.8) | copy-done | bytes 152
  12.0 0.1 dynamic_slice.3.durations_ref
  12.1 0.0 copy-done.7
  12.1 0.1 broadcast_in_dim.9.starts_ref
  12.2 0.0 copy-done.5
  12.2 0.0 copy-done.6
  12.2 1.9 %prepare.1 = (bf16[512,512]{1,0:T(8,128)(2,1)S(1)}, f32[2,512,128]{2,1,0:T(8,128)S(1)}, f32[3,512,128]{2,1,0:T(8,128)S(1)}, bf16[256,1024]{1,0:T(8,128)(2,1)S(1)}) custom-call(s32[16]{0:T(128)S(1)} %dynamic_slice.3.durations_ref, s32[32,128]{1,0:T(8,128)S(1)} %broadcast_in_dim.9.starts_ref, f32[4,512]{1,0:T(4,128)S(1)} %bitcast.9, f32[1,256]{1,0:T(1,128)S(1)} %bitcast.10), custom_call_target="tpu_custom_call" | custom-call | flops 100000000 | bytes 4000000 | tf_op jit(solution)/shard_map/prepare/pallas_call | solution.py:182
  14.1 0.0 copy-start.1
  14.1 0.8 %copy-done.1 = f32[2,512,128]{2,1,0:T(8,128)} copy-done((f32[2,512,128]{2,1,0:T(8,128)}, f32[2,512,128]{2,1,0:T(8,128)S(1)}, u32[]{:S(2)}) %copy-start.1) | copy-done | bytes 524312
  14.9 0.8 %copy-done.3 = bf16[256,1024]{1,0:T(8,128)(2,1)} copy-done((bf16[256,1024]{1,0:T(8,128)(2,1)}, bf16[256,1024]{1,0:T(8,128)(2,1)S(1)}, u32[]{:S(2)}) %copy-start.3) | copy-done | bytes 524312
  15.7 0.0 all-to-all-done.offset_ref
  15.7 1.9 %pick.1 = bf16[512,128]{1,0:T(8,128)(2,1)S(1)} custom-call(s32[1]{0:T(128)} %bitcast.me_ref, s32[8,2,256]{2,1,0:T(2,128)S(1)} %all-to-all-done.offset_ref, bf16[32,4,8192]{2,1,0:T(4,128)(2,1)S(1)} %hold.1.spec_ref), custom_call_target="tpu_custom_call" | custom-call | flops 10000000 | bytes 2097152 | tf_op jit(solution)/shard_map/pick/pallas_call | solution.py:107
  17.6 9.9 %all_to_all.15 = bf16[16,32,128]{2,1,0:T(8,128)(2,1)S(1)} all-to-all(bf16[16,32,128]{2,1,0:T(8,128)(2,1)S(1)} %bitcast.8), channel_id=1, replica_groups={{9,2,4,6,8,10,12,14,1,3,5,7,0,11,13,15},{25,18,20,22,24,26,28,30,17,19,..., dimensions={0} | all-to-all | bytes 262144 | tf_op jit(solution)/shard_map/all_to_all | solution.py:245
  27.5 0.0 copy-done.2
  27.5 0.0 copy-done.4
  27.5 1.8 %statistic.1 = (f32[512,256]{1,0:T(8,128)}, f32[8,16,128]{2,1,0:T(8,128)S(1)}) custom-call(bf16[512,128]{1,0:T(8,128)(2,1)S(1)} %bitcast.7, bf16[512,512]{1,0:T(8,128)(2,1)S(1)} %get-tuple-element.18.mask_ref, f32[2,512,128]{2,1,0:T(8,128)S(1)} %copy-done.2, f32[3,512,128]{2,1,0:T(8,128)S(1)} %get-tuple-element.20.coef_ref, bf16[256,1024]{1,0:T(8,128)(2,1)S(1)} %copy-done.4), custom_call_target="tpu_custom_call" | custom-call | flops 400000000 | bytes 4000000 | tf_op jit(solution)/shard_map/statistic/pallas_call | solution.py:229
  29.3 8.6 %all_to_all.16 = f32[8,16,128]{2,1,0:T(8,128)S(1)} all-to-all(f32[8,16,128]{2,1,0:T(8,128)S(1)} %get-tuple-element.23), channel_id=1, replica_groups={{8,2,4,6,0,10,12,14},{9,3,5,7,1,11,13,15},{24,18,20,22,16,26,28,30},{25..., dimensions={0} | all-to-all | bytes 131072 | tf_op jit(solution)/shard_map/all_to_all | solution.py:245
  37.9 0.6 %slice_reduce_fusion = f32[16,32]{1,0:T(8,128)} fusion(f32[8,16,128]{2,1,0:T(8,128)S(1)} %all_to_all.16), kind=kLoop, calls=%fused_computation | loop fusion | flops 3584 | bytes 18432 | tf_op jit(solution)/shard_map/reduce_max | solution.py:264
  (6 shorter events, 0.0 us)
Async XLA Ops:
  1.9 13.8 %all-to-all-start = ((s32[8,2,256]{2,1,0:T(2,128)}), s32[8,2,256]{2,1,0:T(2,128)S(1)}, u32[]{:S(2)}, u32[]{:S(2)}) async-start(s32[8,2,256]{2,1,0:T(2,128)} %broadcast_in_dim.21), calls=%async_computation | async-start | bytes 32768 | tf_op jit(solution)/shard_map/all_to_all | solution.py:245
  9.8 1.6 %copy-start = (bf16[32,4,8192]{2,1,0:T(4,128)(2,1)S(1)}, bf16[32,4,8192]{2,1,0:T(4,128)(2,1)}, u32[]{:S(2)}) copy-start(bf16[32,4,8192]{2,1,0:T(4,128)(2,1)} %spec_ref.1) | copy-start | bytes 6291460
  11.4 0.7 %copy-start.8 = (s32[32]{0:T(128)S(1)}, s32[32]{0:T(128)}, u32[]{:S(2)}) copy-start(s32[32]{0:T(128)} %param.11) | copy-start | bytes 388
  11.4 0.7 %copy-start.7 = (s32[32]{0:T(128)S(1)}, s32[32]{0:T(128)}, u32[]{:S(2)}) copy-start(s32[32]{0:T(128)} %param.10) | copy-start | bytes 388
  11.4 0.8 %copy-start.5 = (f32[512,4]{0,1:T(4,128)S(1)}, f32[512,4]{0,1:T(4,128)}, u32[]{:S(2)}) copy-start(f32[512,4]{0,1:T(4,128)} %param.9) | copy-start | bytes 24580
  11.4 0.8 %copy-start.6 = (f32[256]{0:T(256)S(1)}, f32[256]{0:T(256)}, u32[]{:S(2)}) copy-start(f32[256]{0:T(256)} %param.8) | copy-start | bytes 3076
  14.1 0.8 %copy-start.1 = (f32[2,512,128]{2,1,0:T(8,128)}, f32[2,512,128]{2,1,0:T(8,128)S(1)}, u32[]{:S(2)}) copy-start(f32[2,512,128]{2,1,0:T(8,128)S(1)} %get-tuple-element.19.weigh_ref) | copy-start | bytes 1572868
  14.9 0.8 %copy-start.3 = (bf16[256,1024]{1,0:T(8,128)(2,1)}, bf16[256,1024]{1,0:T(8,128)(2,1)S(1)}, u32[]{:S(2)}) copy-start(bf16[256,1024]{1,0:T(8,128)(2,1)S(1)} %get-tuple-element.21.kernel_ref) | copy-start | bytes 1572868
  15.7 11.8 %copy-start.2 = (f32[2,512,128]{2,1,0:T(8,128)S(1)}, f32[2,512,128]{2,1,0:T(8,128)}, u32[]{:S(2)}) copy-start(f32[2,512,128]{2,1,0:T(8,128)} %copy-done.1) | copy-start | bytes 1572868
  15.7 11.8 %copy-start.4 = (bf16[256,1024]{1,0:T(8,128)(2,1)S(1)}, bf16[256,1024]{1,0:T(8,128)(2,1)}, u32[]{:S(2)}) copy-start(bf16[256,1024]{1,0:T(8,128)(2,1)} %copy-done.3) | copy-start | bytes 1572868
where the time goes:
time: 38.9 us; the launch traced here: 38.5 us
  blocking collectives  18.5 us (48%)
  starting transfers between devices  7.84 us (20%)
  Pallas kernels  5.76 us (15%)
  local copies, waits for them, and re-layouts  5.11 us (13%)
  between operations  0.68 us (2%)
  other arithmetic  0.61 us (2%)
    all_to_all x2, blocking collectives, exchange(): lax.all_to_all(values, axis, split_axis=0, concat_axis=0, axis_index_grou...  18.5 us
    all_to_all x1, starting transfers between devices, exchange(): lax.all_to_all(values, axis, split_axis=0, concat_axis=0, axis_index_grou...  7.84 us
    unnamed x18, local copies, waits for them, and re-layouts  3.67 us
    pallas_call x1, Pallas kernels, prepare(): pl.pallas_call(functools.partial(prepare_kernel, first, run), out_shape=(...  1.93 us
    pallas_call x1, Pallas kernels, pick(): pl.pallas_call(functools.partial(pick_kernel, bands_in, bands_out), out_s...  1.89 us
    pallas_call x1, Pallas kernels, statistic(): pl.pallas_call(statistic_kernel, out_shape=(jax.ShapeDtypeStruct((count *...  1.79 us
    broadcast_in_dim x1, local copies, waits for them, and re-layouts, body(): jnp.broadcast_to(offsets.T[None], (bands,) + offsets.T.shape)  1.29 us
  transfers between devices with their start and end apart: 1, of which 0 were waited for; matrix products, arithmetic and copies ran while one was open for 0% of the time, Pallas kernels for 5%

commit v1 on v0

--- a/solution.py
+++ b/solution.py
@@ -20,6 +20,25 @@
     members = list(range(size))
     members[0], members[first] = first, 0
     return members
+
+
+def repeat_kernel(in_ref, out_ref, sems):
+    copies = [pltpu.make_async_copy(in_ref, out_ref.at[n], sems.at[n]) for n in range(out_ref.shape[0])]
+    for copy in copies:
+        copy.start()
+    for copy in copies:
+        copy.wait()
+
+
+def repeat(values, count):
+    return pl.pallas_call(
+        repeat_kernel,
+        out_shape=jax.ShapeDtypeStruct((count,) + values.shape, values.dtype),
+        in_specs=[pl.BlockSpec(memory_space=pl.ANY)],
+        out_specs=pl.BlockSpec(memory_space=pl.ANY),
+        scratch_shapes=[pltpu.SemaphoreType.DMA((count,))],
+        name="repeat",
+    )(values)
 
 
 def hold_kernel(spec_ref, out_ref, sem):
@@ -41,7 +60,7 @@
     )(spectra)
 
 
-def pick_kernel(bands_in, bands_out, me_ref, offset_ref, spec_ref, out_ref, place_ref, turn_ref):
+def pick_kernel(bands_in, bands_out, me_ref, offset_ref, spec_ref, out_ref, place_ref, turn_ref, tile_ref, sems):
     rows, _, bins = spec_ref.shape
     bands, blocks, _ = offset_ref.shape
     band_width = bins // bands
@@ -68,7 +87,7 @@
             place = jnp.take_along_axis(places[pair * 8 : pair * 8 + 8], source + band * blocks, axis=1, mode="promise_in_bounds")
             place_ref[band, pair] = place + ((lane & (W - 1)) + lane_group * band_width)
 
-    def step(band, carry):
+    def gather(band):
         for pair in range(4):
             place = place_ref[band, pair]
             lane_id = place & (LANES - 1)
@@ -76,28 +95,45 @@
             tile = jnp.zeros((8, LANES), jnp.float32)
             for group in range(groups):
                 for chunk in range(chunks):
-                    start = pl.multiple_of(band * band_width + chunk * LANES, LANES)
-                    values = spec_ref[pl.ds(group * 8 + pair * 2, 2), :, pl.ds(start, LANES)]
+                    columns = pl.ds(band * band_width + chunk * LANES, LANES)
+                    values = spec_ref[pl.ds(group * 8 + pair * 2, 2), :, columns]
                     values = values.astype(jnp.float32).reshape(8, LANES)
                     moved = jnp.take_along_axis(values, lane_id, axis=1, mode="promise_in_bounds")
                     tile = jnp.where(chosen == group * chunks + chunk, moved, tile)
             turn_ref[band, pl.ds(pair * 8, 8), :] = tile
-        return carry
-
-    lax.fori_loop(0, bands, step, 0, unroll=2)
-    tiles = {}
-    for band in range(bands):
+
+    def turn(band):
         parts = [turn_ref[band, pl.ds(part, 8, stride=4), :] for part in range(4)]
+        tiles = []
         for group in range(groups):
             tile = jnp.zeros((8, LANES), jnp.float32)
             for part in range(4):
                 amount = (part - group) * width % LANES
                 turned = pltpu.roll(parts[part], amount, 1) if amount else parts[part]
                 tile = jnp.where(lane_group == part, turned, tile)
-            tiles[band, group] = tile
-    wanted = [tiles[band, group] for band in bands_out for group in range(groups)]
-    for n in range(0, len(wanted), 2):
-        out_ref[n * 8 : n * 8 + 16, :] = jnp.concatenate(wanted[n : n + 2], axis=0).astype(jnp.bfloat16)
+            tiles.append(tile)
+        return tiles
+
+    tiles, copies = {}, []
+    for band in range(bands):
+        gather(band)
+        tiles[band] = turn(band)
+        if rows % 16 == 0:
+            here = pl.ds(band * rows, rows)
+            tile_ref[here, :] = jnp.concatenate(tiles[band], axis=0).astype(jnp.bfloat16)
+            for slot in range(len(bands_out)):
+                if bands_out[slot] == band:
+                    there = out_ref.at[pl.ds(slot * rows, rows), :]
+                    copies.append(pltpu.make_async_copy(tile_ref.at[here, :], there, sems.at[slot]))
+                    copies[-1].start()
+    if rows % 16:
+        wanted = [tile for band in bands_out for tile in tiles[band]]
+        for n in range(0, len(wanted), 2):
+            tile_ref[n * 8 : n * 8 + 16, :] = jnp.concatenate(wanted[n : n + 2], axis=0).astype(jnp.bfloat16)
+        copies.append(pltpu.make_async_copy(tile_ref, out_ref, sems.at[0]))
+        copies[-1].start()
+    for copy in copies:
+        copy.wait()
 
 
 def pick(me, offsets, spectra, bands_in, bands_out):
@@ -108,10 +144,12 @@
         functools.partial(pick_kernel, bands_in, bands_out),
         out_shape=jax.ShapeDtypeStruct((out_rows, LANES), jnp.bfloat16),
         in_specs=[pl.BlockSpec(memory_space=pltpu.SMEM), vmem, vmem],
-        out_specs=vmem,
+        out_specs=pl.BlockSpec(memory_space=pl.ANY),
         scratch_shapes=[
             pltpu.VMEM((bands, 4, 8, LANES), jnp.int32),
             pltpu.VMEM((bands, 32, LANES), jnp.float32),
+            pltpu.VMEM((out_rows, LANES), jnp.bfloat16),
+            pltpu.SemaphoreType.DMA((len(bands_out),)),
         ],
         compiler_params=pltpu.CompilerParams(vmem_limit_bytes=8 * 1024 * 1024),
         cost_estimate=pl.CostEstimate(flops=10_000_000, bytes_accessed=2 * spectra.size, transcendentals=0),
@@ -254,11 +292,11 @@
     by_band = order(bands, bands // 2)
     first = (cores - 1) * bands + bands // 2
     by_run = order(cores * bands, first)
-    known = exchange(jnp.broadcast_to(offsets.T[None], (bands,) + offsets.T.shape), "tmpl", by_band)
+    known = exchange(repeat(offsets.T, bands), "tmpl", by_band)
     my_durations = lax.dynamic_slice_in_dim(durations, lax.axis_index("tm") * my_rows, my_rows, 0)
+    windows = pick(me, known, hold(spectra), by_band, [run % bands for run in by_run])
+    windows, my_durations = lax.optimization_barrier((windows, my_durations))
     prepared = prepare(my_durations, starts, antenna, fractions, first, sft_rows)
-    me, prepared = lax.optimization_barrier((me, prepared))
-    windows = pick(me, known, hold(spectra), by_band, [run % bands for run in by_run])
     arrived = exchange(windows.reshape(cores * bands, sft_rows, LANES), ("tm", "tmpl"), by_run)
     fstat_map, loudest = statistic(arrived.reshape(-1, LANES), *prepared, grid_size, bands)
     loudest = jnp.max(exchange(loudest, "tmpl", by_band)[:, :, :grid_size], axis=0)

time: 38.9 us -> 37.2 us (0.956)
  blocking collectives: 18.5 us -> 8.59 us
  waiting for transfers between devices: 0.01 us -> 5.13 us
  starting transfers between devices: 7.84 us -> 11.8 us
  local copies, waits for them, and re-layouts: 5.11 us -> 2.21 us
  Pallas kernels: 5.76 us -> 7.81 us
    all_to_all x2 -> x1, blocking collectives: 18.5 us -> 8.59 us  [exchange(): lax.all_to_all(values, axis, split_axis=0, concat_axis=0, axis_index_grou...]
    all_to_all x1 -> x2, waiting for transfers between devices: 0.01 us -> 5.13 us  [exchange(): lax.all_to_all(values, axis, split_axis=0, concat_axis=0, axis_index_grou...]
    all_to_all x1 -> x2, starting transfers between devices: 7.84 us -> 11.8 us  [exchange(): lax.all_to_all(values, axis, split_axis=0, concat_axis=0, axis_index_grou...]
    pallas_call x0 -> x1, Pallas kernels: none -> 1.67 us  [repeat(): pl.pallas_call(repeat_kernel, out_shape=jax.ShapeDtypeStruct((count,) + v...]
    unnamed x18 -> x10, local copies, waits for them, and re-layouts: 3.67 us -> 2.07 us
    broadcast_in_dim x1 -> x0, local copies, waits for them, and re-layouts: 1.29 us -> none  [body(): jnp.broadcast_to(offsets.T[None], (bands,) + offsets.T.shape)]
  transfers between devices with their start and end apart: 1 -> 2, of which waited for: 0 -> 2; matrix products, arithmetic and copies ran while one was open for 0% -> 0% of each run, Pallas kernels for 5% -> 6%
where the time goes in v1:
time: 37.2 us; the launch traced here: 36.9 us
  starting transfers between devices  11.8 us (32%)
  blocking collectives  8.59 us (23%)
  Pallas kernels  7.81 us (21%)
  waiting for transfers between devices  5.13 us (14%)
  local copies, waits for them, and re-layouts  2.21 us (6%)
  between operations  0.7 us (2%)
  other arithmetic  0.61 us (2%)
    all_to_all x2, starting transfers between devices, exchange(): lax.all_to_all(values, axis, split_axis=0, concat_axis=0, axis_index_grou...  11.8 us
    all_to_all x1, blocking collectives, exchange(): lax.all_to_all(values, axis, split_axis=0, concat_axis=0, axis_index_grou...  8.59 us
    all_to_all x2, waiting for transfers between devices, exchange(): lax.all_to_all(values, axis, split_axis=0, concat_axis=0, axis_index_grou...  5.13 us
    pallas_call x1, Pallas kernels, pick(): pl.pallas_call(functools.partial(pick_kernel, bands_in, bands_out), out_s...  2.27 us
    unnamed x10, local copies, waits for them, and re-layouts  2.07 us
    pallas_call x1, Pallas kernels, prepare(): pl.pallas_call(functools.partial(prepare_kernel, first, run), out_shape=(...  1.93 us
    pallas_call x1, Pallas kernels, statistic(): pl.pallas_call(statistic_kernel, out_shape=(jax.ShapeDtypeStruct((count *...  1.8 us
    pallas_call x1, Pallas kernels, repeat(): pl.pallas_call(repeat_kernel, out_shape=jax.ShapeDtypeStruct((count,) + v...  1.67 us
  transfers between devices with their start and end apart: 2, of which 2 were waited for; matrix products, arithmetic and copies ran while one was open for 0% of the time, Pallas kernels for 6%

profile of v1, /device:TPU:0, one launch (start us, length us, event | category | flops | bytes accessed | tf_op | source)
XLA Modules:
  0.0 36.9 jit_solution(2786537066207928737)
XLA Ops:
  0.6 1.7 %repeat.1 = s32[8,2,256]{2,1,0:T(2,128)} custom-call(s32[2,256]{1,0:T(2,128)} %bitcast.10), custom_call_target="tpu_custom_call" | custom-call | tf_op jit(solution)/shard_map/repeat/pallas_call | solution.py:34
  2.3 7.9 %all-to-all-start = ((s32[8,2,256]{2,1,0:T(2,128)}), s32[8,2,256]{2,1,0:T(2,128)S(1)}, u32[]{:S(2)}, u32[]{:S(2)}) async-start(s32[8,2,256]{2,1,0:T(2,128)} %repeat.1), calls=%async_computation | async-start | bytes 32768 | tf_op jit(solution)/shard_map/all_to_all | solution.py:283
  10.2 0.0 copy-start
  10.2 1.6 %copy-done = bf16[32,4,8192]{2,1,0:T(4,128)(2,1)S(1)} copy-done((bf16[32,4,8192]{2,1,0:T(4,128)(2,1)S(1)}, bf16[32,4,8192]{2,1,0:T(4,128)(2,1)}, u32[]{:S(2)}) %copy-start) | copy-done | bytes 2097176
  11.8 0.0 copy-start.4
  11.8 0.1 hold.1.spec_ref
  11.9 0.0 copy-start.3
  11.9 0.0 copy-start.1
  11.9 0.0 copy-start.2
  11.9 0.5 %copy-done.4 = s32[32]{0:T(128)S(1)} copy-done((s32[32]{0:T(128)S(1)}, s32[32]{0:T(128)}, u32[]{:S(2)}) %copy-start.4) | copy-done | bytes 152
  12.4 0.1 dynamic_slice.3.durations_ref
  12.5 1.9 %all-to-all-done.offset_ref = s32[8,2,256]{2,1,0:T(2,128)S(1)} async-done(((s32[8,2,256]{2,1,0:T(2,128)}), s32[8,2,256]{2,1,0:T(2,128)S(1)}, u32[]{:S(2)}, u32[]{:S(2)}) %all-to-all-start) | async-done | bytes 16416 | tf_op jit(solution)/shard_map/all_to_all | solution.py:283
  14.4 2.3 %pick.1 = bf16[512,128]{1,0:T(8,128)(2,1)} custom-call(s32[1]{0:T(128)} %bitcast.me_ref, s32[8,2,256]{2,1,0:T(2,128)S(1)} %all-to-all-done.offset_ref, bf16[32,4,8192]{2,1,0:T(4,128)(2,1)S(1)} %hold.1.spec_ref), custom_call_target="tpu_custom_call" | custom-call | flops 10000000 | bytes 2097152 | tf_op jit(solution)/shard_map/pick/pallas_call | solution.py:143
  16.6 4.0 %all-to-all-start.1 = ((bf16[16,32,128]{2,1,0:T(8,128)(2,1)}), bf16[16,32,128]{2,1,0:T(8,128)(2,1)S(1)}, u32[]{:S(2)}, u32[]{:S(2)}) async-start(bf16[16,32,128]{2,1,0:T(8,128)(2,1)} %bitcast.2), calls=%async_computation.1 | async-start | bytes 262144 | tf_op jit(solution)/shard_map/all_to_all | solution.py:283
  20.6 0.0 copy-done.3
  20.6 0.1 broadcast_in_dim.13.starts_ref
  20.7 0.0 copy-done.1
  20.7 0.0 copy-done.2
  20.7 1.9 %prepare.1 = (bf16[512,512]{1,0:T(8,128)(2,1)S(1)}, f32[2,512,128]{2,1,0:T(8,128)S(1)}, f32[3,512,128]{2,1,0:T(8,128)S(1)}, bf16[256,1024]{1,0:T(8,128)(2,1)S(1)}) custom-call(s32[16]{0:T(128)S(1)} %dynamic_slice.3.durations_ref, s32[32,128]{1,0:T(8,128)S(1)} %broadcast_in_dim.13.starts_ref, f32[4,512]{1,0:T(4,128)S(1)} %bitcast.8, f32[1,256]{1,0:T(1,128)S(1)} %bitcast.9), custom_call_target="tpu_custom_call" | custom-call | flops 100000000 | bytes 4000000 | tf_op jit(solution)/shard_map/prepare/pallas_call | solution.py:220
  22.6 3.3 %all-to-all-done.1 = bf16[16,32,128]{2,1,0:T(8,128)(2,1)S(1)} async-done(((bf16[16,32,128]{2,1,0:T(8,128)(2,1)}), bf16[16,32,128]{2,1,0:T(8,128)(2,1)S(1)}, u32[]{:S(2)}, u32[]{:S(2)}) %all-to-all-start.1) | async-done | bytes 131104 | tf_op jit(solution)/shard_map/all_to_all | solution.py:283
  25.9 1.8 %statistic.1 = (f32[512,256]{1,0:T(8,128)}, f32[8,16,128]{2,1,0:T(8,128)S(1)}) custom-call(bf16[512,128]{1,0:T(8,128)(2,1)S(1)} %bitcast.7, bf16[512,512]{1,0:T(8,128)(2,1)S(1)} %get-tuple-element.12.mask_ref, f32[2,512,128]{2,1,0:T(8,128)S(1)} %get-tuple-element.13.weigh_ref, f32[3,512,128]{2,1,0:T(8,128)S(1)} %get-tuple-element.14.coef_ref, ...), custom_call_target="tpu_custom_call" | custom-call | flops 400000000 | bytes 4000000 | tf_op jit(solution)/shard_map/statistic/pallas_call | solution.py:267
  27.7 8.6 %all_to_all.15 = f32[8,16,128]{2,1,0:T(8,128)S(1)} all-to-all(f32[8,16,128]{2,1,0:T(8,128)S(1)} %get-tuple-element.17), channel_id=1, replica_groups={{8,2,4,6,0,10,12,14},{9,3,5,7,1,11,13,15},{24,18,20,22,16,26,28,30},{25..., dimensions={0} | all-to-all | bytes 131072 | tf_op jit(solution)/shard_map/all_to_all | solution.py:283
  36.3 0.6 %slice_reduce_fusion = f32[16,32]{1,0:T(8,128)} fusion(f32[8,16,128]{2,1,0:T(8,128)S(1)} %all_to_all.15), kind=kLoop, calls=%fused_computation | loop fusion | flops 3584 | bytes 18432 | tf_op jit(solution)/shard_map/reduce_max | solution.py:302
Async XLA Ops:
  2.3 12.0 %all-to-all-start = ((s32[8,2,256]{2,1,0:T(2,128)}), s32[8,2,256]{2,1,0:T(2,128)S(1)}, u32[]{:S(2)}, u32[]{:S(2)}) async-start(s32[8,2,256]{2,1,0:T(2,128)} %repeat.1), calls=%async_computation | async-start | bytes 32768 | tf_op jit(solution)/shard_map/all_to_all | solution.py:283
  10.2 1.6 %copy-start = (bf16[32,4,8192]{2,1,0:T(4,128)(2,1)S(1)}, bf16[32,4,8192]{2,1,0:T(4,128)(2,1)}, u32[]{:S(2)}) copy-start(bf16[32,4,8192]{2,1,0:T(4,128)(2,1)} %spec_ref.1) | copy-start | bytes 6291460
  11.8 0.7 %copy-start.4 = (s32[32]{0:T(128)S(1)}, s32[32]{0:T(128)}, u32[]{:S(2)}) copy-start(s32[32]{0:T(128)} %param.11) | copy-start | bytes 388
  11.9 8.7 %copy-start.3 = (s32[32]{0:T(128)S(1)}, s32[32]{0:T(128)}, u32[]{:S(2)}) copy-start(s32[32]{0:T(128)} %param.10) | copy-start | bytes 388
  11.9 8.8 %copy-start.1 = (f32[512,4]{0,1:T(4,128)S(1)}, f32[512,4]{0,1:T(4,128)}, u32[]{:S(2)}) copy-start(f32[512,4]{0,1:T(4,128)} %param.9) | copy-start | bytes 24580
  11.9 8.8 %copy-start.2 = (f32[256]{0:T(256)S(1)}, f32[256]{0:T(256)}, u32[]{:S(2)}) copy-start(f32[256]{0:T(256)} %param.8) | copy-start | bytes 3076
  16.6 9.3 %all-to-all-start.1 = ((bf16[16,32,128]{2,1,0:T(8,128)(2,1)}), bf16[16,32,128]{2,1,0:T(8,128)(2,1)S(1)}, u32[]{:S(2)}, u32[]{:S(2)}) async-start(bf16[16,32,128]{2,1,0:T(8,128)(2,1)} %bitcast.2), calls=%async_computation.1 | async-start | bytes 262144 | tf_op jit(solution)/shard_map/all_to_all | solution.py:283

commit v2 on v1

--- a/solution.py
+++ b/solution.py
@@ -20,44 +20,6 @@
     members = list(range(size))
     members[0], members[first] = first, 0
     return members
-
-
-def repeat_kernel(in_ref, out_ref, sems):
-    copies = [pltpu.make_async_copy(in_ref, out_ref.at[n], sems.at[n]) for n in range(out_ref.shape[0])]
-    for copy in copies:
-        copy.start()
-    for copy in copies:
-        copy.wait()
-
-
-def repeat(values, count):
-    return pl.pallas_call(
-        repeat_kernel,
-        out_shape=jax.ShapeDtypeStruct((count,) + values.shape, values.dtype),
-        in_specs=[pl.BlockSpec(memory_space=pl.ANY)],
-        out_specs=pl.BlockSpec(memory_space=pl.ANY),
-        scratch_shapes=[pltpu.SemaphoreType.DMA((count,))],
-        name="repeat",
-    )(values)
-
-
-def hold_kernel(spec_ref, out_ref, sem):
-    copy = pltpu.make_async_copy(spec_ref, out_ref, sem)
-    copy.start()
-    copy.wait()
-
-
-def hold(spectra):
-    return pl.pallas_call(
-        hold_kernel,
-        out_shape=jax.ShapeDtypeStruct(spectra.shape, spectra.dtype),
-        in_specs=[pl.BlockSpec(memory_space=pl.ANY)],
-        out_specs=pl.BlockSpec(memory_space=pltpu.VMEM),
-        scratch_shapes=[pltpu.SemaphoreType.DMA],
-        compiler_params=pltpu.CompilerParams(vmem_limit_bytes=8 * 1024 * 1024),
-        cost_estimate=pl.CostEstimate(flops=0, bytes_accessed=4 * spectra.size, transcendentals=0),
-        name="hold",
-    )(spectra)
 
 
 def pick_kernel(bands_in, bands_out, me_ref, offset_ref, spec_ref, out_ref, place_ref, turn_ref, tile_ref, sems):
@@ -292,10 +254,11 @@
     by_band = order(bands, bands // 2)
     first = (cores - 1) * bands + bands // 2
     by_run = order(cores * bands, first)
-    known = exchange(repeat(offsets.T, bands), "tmpl", by_band)
+    known = exchange(jnp.broadcast_to(offsets.T[None], (bands,) + offsets.T.shape), "tmpl", by_band)
+    windows = pick(me, known, spectra, by_band, [run % bands for run in by_run])
+    windows, *late = lax.optimization_barrier((windows, durations, starts, antenna, fractions))
+    durations, starts, antenna, fractions = late
     my_durations = lax.dynamic_slice_in_dim(durations, lax.axis_index("tm") * my_rows, my_rows, 0)
-    windows = pick(me, known, hold(spectra), by_band, [run % bands for run in by_run])
-    windows, my_durations = lax.optimization_barrier((windows, my_durations))
     prepared = prepare(my_durations, starts, antenna, fractions, first, sft_rows)
     arrived = exchange(windows.reshape(cores * bands, sft_rows, LANES), ("tm", "tmpl"), by_run)
     fstat_map, loudest = statistic(arrived.reshape(-1, LANES), *prepared, grid_size, bands)

time: 37.2 us -> 38.5 us (1.035)
  waiting for transfers between devices: 5.13 us -> 7.38 us
  Pallas kernels: 7.81 us -> 6 us
  local copies, waits for them, and re-layouts: 2.21 us -> 3.07 us
    all_to_all x2, waiting for transfers between devices: 5.13 us -> 7.38 us  [exchange(): lax.all_to_all(values, axis, split_axis=0, concat_axis=0, axis_index_grou...]
    pallas_call x2 -> x0, Pallas kernels: 1.82 us -> none  [the longest x1 1.67 us: repeat(): pl.pallas_call(repeat_kernel, out_shape=jax.ShapeDtypeStruct((count,) + v...]
    broadcast_in_dim x0 -> x1, local copies, waits for them, and re-layouts: none -> 1.31 us  [body(): jnp.broadcast_to(offsets.T[None], (bands,) + offsets.T.shape)]
    unnamed x10, local copies, waits for them, and re-layouts: 2.07 us -> 1.61 us
  transfers between devices with their start and end apart: 2 -> 2, of which waited for: 2 -> 2; matrix products, arithmetic and copies ran while one was open for 0% -> 0% of each run, Pallas kernels for 6% -> 5%
where the time goes in v2:
time: 38.5 us; the launch traced here: 38.2 us
  starting transfers between devices  11.8 us (31%)
  blocking collectives  8.59 us (22%)
  waiting for transfers between devices  7.38 us (19%)
  Pallas kernels  6 us (16%)
  local copies, waits for them, and re-layouts  3.07 us (8%)
  between operations  0.69 us (2%)
  other arithmetic  0.61 us (2%)
    all_to_all x2, starting transfers between devices, exchange(): lax.all_to_all(values, axis, split_axis=0, concat_axis=0, axis_index_grou...  11.8 us
    all_to_all x1, blocking collectives, exchange(): lax.all_to_all(values, axis, split_axis=0, concat_axis=0, axis_index_grou...  8.59 us
    all_to_all x2, waiting for transfers between devices, exchange(): lax.all_to_all(values, axis, split_axis=0, concat_axis=0, axis_index_grou...  7.38 us
    pallas_call x1, Pallas kernels, pick(): pl.pallas_call(functools.partial(pick_kernel, bands_in, bands_out), out_s...  2.28 us
    pallas_call x1, Pallas kernels, prepare(): pl.pallas_call(functools.partial(prepare_kernel, first, run), out_shape=(...  1.93 us
    pallas_call x1, Pallas kernels, statistic(): pl.pallas_call(statistic_kernel, out_shape=(jax.ShapeDtypeStruct((count *...  1.79 us
    unnamed x10, local copies, waits for them, and re-layouts  1.61 us
    broadcast_in_dim x1, local copies, waits for them, and re-layouts, body(): jnp.broadcast_to(offsets.T[None], (bands,) + offsets.T.shape)  1.31 us
  transfers between devices with their start and end apart: 2, of which 2 were waited for; matrix products, arithmetic and copies ran while one was open for 0% of the time, Pallas kernels for 5%

profile of v2, /device:TPU:0, one launch (start us, length us, event | category | flops | bytes accessed | tf_op | source)
XLA Modules:
  0.0 38.2 jit_solution(14813606924707480262)
XLA Ops:
  0.6 0.0 copy-start.4
  0.6 0.0 copy-start.3
  0.7 0.0 copy-start.1
  0.7 0.0 copy-start.2
  0.7 1.3 %broadcast_in_dim.9 = s32[8,2,256]{2,1,0:T(2,128)} broadcast(s32[2,256]{1,0:T(2,128)} %bitcast.10), dimensions={1,2} | broadcast | bytes 18432 | tf_op jit(solution)/shard_map/broadcast_in_dim | solution.py:257
  2.0 7.8 %all-to-all-start = ((s32[8,2,256]{2,1,0:T(2,128)}), s32[8,2,256]{2,1,0:T(2,128)S(1)}, u32[]{:S(2)}, u32[]{:S(2)}) async-start(s32[8,2,256]{2,1,0:T(2,128)} %broadcast_in_dim.9), calls=%async_computation | async-start | bytes 32768 | tf_op jit(solution)/shard_map/all_to_all | solution.py:245
  9.8 4.2 %all-to-all-done.offset_ref = s32[8,2,256]{2,1,0:T(2,128)S(1)} async-done(((s32[8,2,256]{2,1,0:T(2,128)}), s32[8,2,256]{2,1,0:T(2,128)S(1)}, u32[]{:S(2)}, u32[]{:S(2)}) %all-to-all-start) | async-done | bytes 16416 | tf_op jit(solution)/shard_map/all_to_all | solution.py:245
  14.0 0.0 copy-start
  14.0 1.6 %copy-done = bf16[32,4,8192]{2,1,0:T(4,128)(2,1)S(1)} copy-done((bf16[32,4,8192]{2,1,0:T(4,128)(2,1)S(1)}, bf16[32,4,8192]{2,1,0:T(4,128)(2,1)}, u32[]{:S(2)}) %copy-start) | copy-done | bytes 2097176
  15.6 2.3 %pick.1 = bf16[512,128]{1,0:T(8,128)(2,1)} custom-call(s32[1]{0:T(128)} %bitcast.me_ref, s32[8,2,256]{2,1,0:T(2,128)S(1)} %all-to-all-done.offset_ref, bf16[32,4,8192]{2,1,0:T(4,128)(2,1)S(1)} %copy-done), custom_call_target="tpu_custom_call" | custom-call | flops 10000000 | bytes 2097152 | tf_op jit(solution)/shard_map/pick/pallas_call | solution.py:105
  17.9 4.0 %all-to-all-start.1 = ((bf16[16,32,128]{2,1,0:T(8,128)(2,1)}), bf16[16,32,128]{2,1,0:T(8,128)(2,1)S(1)}, u32[]{:S(2)}, u32[]{:S(2)}) async-start(bf16[16,32,128]{2,1,0:T(8,128)(2,1)} %bitcast.2), calls=%async_computation.1 | async-start | bytes 262144 | tf_op jit(solution)/shard_map/all_to_all | solution.py:245
  21.9 0.0 copy-done.4
  21.9 0.1 dynamic_slice.3.durations_ref
  22.0 0.0 copy-done.3
  22.0 0.1 broadcast_in_dim.20.starts_ref
  22.0 0.0 copy-done.1
  22.0 0.0 copy-done.2
  22.1 1.9 %prepare.1 = (bf16[512,512]{1,0:T(8,128)(2,1)S(1)}, f32[2,512,128]{2,1,0:T(8,128)S(1)}, f32[3,512,128]{2,1,0:T(8,128)S(1)}, bf16[256,1024]{1,0:T(8,128)(2,1)S(1)}) custom-call(s32[16]{0:T(128)S(1)} %dynamic_slice.3.durations_ref, s32[32,128]{1,0:T(8,128)S(1)} %broadcast_in_dim.20.starts_ref, f32[4,512]{1,0:T(4,128)S(1)} %bitcast.8, f32[1,256]{1,0:T(1,128)S(1)} %bitcast.9), custom_call_target="tpu_custom_call" | custom-call | flops 100000000 | bytes 4000000 | tf_op jit(solution)/shard_map/prepare/pallas_call | solution.py:182
  24.0 3.2 %all-to-all-done.1 = bf16[16,32,128]{2,1,0:T(8,128)(2,1)S(1)} async-done(((bf16[16,32,128]{2,1,0:T(8,128)(2,1)}), bf16[16,32,128]{2,1,0:T(8,128)(2,1)S(1)}, u32[]{:S(2)}, u32[]{:S(2)}) %all-to-all-start.1) | async-done | bytes 131104 | tf_op jit(solution)/shard_map/all_to_all | solution.py:245
  27.2 1.8 %statistic.1 = (f32[512,256]{1,0:T(8,128)}, f32[8,16,128]{2,1,0:T(8,128)S(1)}) custom-call(bf16[512,128]{1,0:T(8,128)(2,1)S(1)} %bitcast.7, bf16[512,512]{1,0:T(8,128)(2,1)S(1)} %get-tuple-element.18.mask_ref, f32[2,512,128]{2,1,0:T(8,128)S(1)} %get-tuple-element.19.weigh_ref, f32[3,512,128]{2,1,0:T(8,128)S(1)} %get-tuple-element.20.coef_ref, ...), custom_call_target="tpu_custom_call" | custom-call | flops 400000000 | bytes 4000000 | tf_op jit(solution)/shard_map/statistic/pallas_call | solution.py:229
  29.0 8.6 %all_to_all.15 = f32[8,16,128]{2,1,0:T(8,128)S(1)} all-to-all(f32[8,16,128]{2,1,0:T(8,128)S(1)} %get-tuple-element.23), channel_id=1, replica_groups={{8,2,4,6,0,10,12,14},{9,3,5,7,1,11,13,15},{24,18,20,22,16,26,28,30},{25..., dimensions={0} | all-to-all | bytes 131072 | tf_op jit(solution)/shard_map/all_to_all | solution.py:245
  37.5 0.6 %slice_reduce_fusion = f32[16,32]{1,0:T(8,128)} fusion(f32[8,16,128]{2,1,0:T(8,128)S(1)} %all_to_all.15), kind=kLoop, calls=%fused_computation | loop fusion | flops 3584 | bytes 18432 | tf_op jit(solution)/shard_map/reduce_max | solution.py:265
Async XLA Ops:
  0.6 21.3 %copy-start.4 = (s32[32]{0:T(128)S(1)}, s32[32]{0:T(128)}, u32[]{:S(2)}) copy-start(s32[32]{0:T(128)} %param.11) | copy-start | bytes 388
  0.6 21.3 %copy-start.3 = (s32[32]{0:T(128)S(1)}, s32[32]{0:T(128)}, u32[]{:S(2)}) copy-start(s32[32]{0:T(128)} %param.10) | copy-start | bytes 388
  0.7 21.4 %copy-start.1 = (f32[512,4]{0,1:T(4,128)S(1)}, f32[512,4]{0,1:T(4,128)}, u32[]{:S(2)}) copy-start(f32[512,4]{0,1:T(4,128)} %param.9) | copy-start | bytes 24580
  0.7 21.4 %copy-start.2 = (f32[256]{0:T(256)S(1)}, f32[256]{0:T(256)}, u32[]{:S(2)}) copy-start(f32[256]{0:T(256)} %param.8) | copy-start | bytes 3076
  2.0 12.0 %all-to-all-start = ((s32[8,2,256]{2,1,0:T(2,128)}), s32[8,2,256]{2,1,0:T(2,128)S(1)}, u32[]{:S(2)}, u32[]{:S(2)}) async-start(s32[8,2,256]{2,1,0:T(2,128)} %broadcast_in_dim.9), calls=%async_computation | async-start | bytes 32768 | tf_op jit(solution)/shard_map/all_to_all | solution.py:245
  14.0 1.6 %copy-start = (bf16[32,4,8192]{2,1,0:T(4,128)(2,1)S(1)}, bf16[32,4,8192]{2,1,0:T(4,128)(2,1)}, u32[]{:S(2)}) copy-start(bf16[32,4,8192]{2,1,0:T(4,128)(2,1)} %spec_ref.1) | copy-start | bytes 6291460
  17.9 9.3 %all-to-all-start.1 = ((bf16[16,32,128]{2,1,0:T(8,128)(2,1)}), bf16[16,32,128]{2,1,0:T(8,128)(2,1)S(1)}, u32[]{:S(2)}, u32[]{:S(2)}) async-start(bf16[16,32,128]{2,1,0:T(8,128)(2,1)} %bitcast.2), calls=%async_computation.1 | async-start | bytes 262144 | tf_op jit(solution)/shard_map/all_to_all | solution.py:245

commit v3 on v2

--- a/solution.py
+++ b/solution.py
@@ -22,14 +22,14 @@
     return members
 
 
-def pick_kernel(bands_in, bands_out, me_ref, offset_ref, spec_ref, out_ref, place_ref, turn_ref, tile_ref, sems):
+def pick_kernel(bands_in, bands_out, offset_ref, spec_ref, out_ref, place_ref, turn_ref, tile_ref, sems):
     rows, _, bins = spec_ref.shape
     bands, blocks, _ = offset_ref.shape
     band_width = bins // bands
     groups = rows // 8
     chunks = band_width // LANES
     width = blocks * W
-    first = me_ref[0] * rows
+    first = lax.axis_index("tmpl").astype(jnp.int32) * rows
     columns = pl.ds(pl.multiple_of(first // LANES * LANES, LANES), LANES)
     offsets = jnp.concatenate([offset_ref[bands_in.index(band), :, columns] for band in range(bands)], axis=0).astype(jnp.float32)
     lane = iota(offsets.shape, 1)
@@ -98,14 +98,14 @@
         copy.wait()
 
 
-def pick(me, offsets, spectra, bands_in, bands_out):
+def pick(offsets, spectra, bands_in, bands_out):
     rows, bands = spectra.shape[0], offsets.shape[0]
     out_rows = len(bands_out) * rows
     vmem = pl.BlockSpec(memory_space=pltpu.VMEM)
     return pl.pallas_call(
         functools.partial(pick_kernel, bands_in, bands_out),
         out_shape=jax.ShapeDtypeStruct((out_rows, LANES), jnp.bfloat16),
-        in_specs=[pl.BlockSpec(memory_space=pltpu.SMEM), vmem, vmem],
+        in_specs=[vmem, vmem],
         out_specs=pl.BlockSpec(memory_space=pl.ANY),
         scratch_shapes=[
             pltpu.VMEM((bands, 4, 8, LANES), jnp.int32),
@@ -116,7 +116,7 @@
         compiler_params=pltpu.CompilerParams(vmem_limit_bytes=8 * 1024 * 1024),
         cost_estimate=pl.CostEstimate(flops=10_000_000, bytes_accessed=2 * spectra.size, transcendentals=0),
         name="pick",
-    )(me, offsets, spectra)
+    )(offsets, spectra)
 
 
 def split(values, count):
@@ -130,14 +130,15 @@
 
 def prepare_kernel(first, run, durations_ref, starts_ref, antenna_ref, fractions_ref, mask_ref, weigh_ref, coef_ref, kernel_ref):
     rows = starts_ref.shape[0]
-    count = durations_ref.shape[0]
+    count = mask_ref.shape[0] // rows
+    mine = lax.axis_index("tm").astype(jnp.int32) * count
     sfts = antenna_ref.shape[1]
     sft = iota((rows, sfts), 1)
     sft = jnp.where(sft // run == 0, sft + first * run, jnp.where(sft // run == first, sft - first * run, sft))
     start = starts_ref[:, 0:1]
     after = sft >= start
     for j in range(count):
-        inside = after & (sft < start + durations_ref[j])
+        inside = after & (sft < start + durations_ref[mine + j])
         mask_ref[pl.ds(j * rows, rows), :] = jnp.where(inside, 1.0, 0.0).astype(jnp.bfloat16)
     antenna = jnp.concatenate([antenna_ref[...], jnp.zeros((4, sfts), jnp.float32)], axis=0)
     place = iota(antenna.shape, 1) // run
@@ -174,8 +175,8 @@
                 kernel_ref[pl.ds(row, W), pl.ds(column, LANES)] = values[:, b * LANES : (b + 1) * LANES]
 
 
-def prepare(durations, starts, antenna, fractions, first, run):
-    count, rows, sfts = durations.shape[0], starts.shape[0], antenna.shape[0]
+def prepare(durations, starts, antenna, fractions, first, run, cores):
+    count, rows, sfts = durations.shape[0] // cores, starts.shape[0], antenna.shape[0]
     columns = 4 * fractions.shape[0]
     features = 4 * W * (fractions.shape[0] // LANES)
     vmem = pl.BlockSpec(memory_space=pltpu.VMEM)
@@ -250,16 +251,14 @@
     sft_rows = spectra.shape[0]
     grid_size = starts.shape[0]
     my_rows = grid_size // cores
-    me = lax.axis_index("tmpl").astype(jnp.int32)[None]
     by_band = order(bands, bands // 2)
     first = (cores - 1) * bands + bands // 2
     by_run = order(cores * bands, first)
     known = exchange(jnp.broadcast_to(offsets.T[None], (bands,) + offsets.T.shape), "tmpl", by_band)
-    windows = pick(me, known, spectra, by_band, [run % bands for run in by_run])
+    windows = pick(known, spectra, by_band, [run % bands for run in by_run])
     windows, *late = lax.optimization_barrier((windows, durations, starts, antenna, fractions))
     durations, starts, antenna, fractions = late
-    my_durations = lax.dynamic_slice_in_dim(durations, lax.axis_index("tm") * my_rows, my_rows, 0)
-    prepared = prepare(my_durations, starts, antenna, fractions, first, sft_rows)
+    prepared = prepare(durations, starts, antenna, fractions, first, sft_rows, cores)
     arrived = exchange(windows.reshape(cores * bands, sft_rows, LANES), ("tm", "tmpl"), by_run)
     fstat_map, loudest = statistic(arrived.reshape(-1, LANES), *prepared, grid_size, bands)
     loudest = jnp.max(exchange(loudest, "tmpl", by_band)[:, :, :grid_size], axis=0)

time: 38.5 us -> 37.6 us (0.977)
  blocking collectives: 8.59 us -> 20.4 us
  starting transfers between devices: 11.8 us -> 3.98 us
  waiting for transfers between devices: 7.38 us -> 3.26 us
  local copies, waits for them, and re-layouts: 3.07 us -> 2.39 us
    all_to_all x1 -> x2, blocking collectives: 8.59 us -> 20.4 us  [exchange(): lax.all_to_all(values, axis, split_axis=0, concat_axis=0, axis_index_grou...]
    all_to_all x2 -> x1, starting transfers between devices: 11.8 us -> 3.98 us  [exchange(): lax.all_to_all(values, axis, split_axis=0, concat_axis=0, axis_index_grou...]
    all_to_all x2 -> x1, waiting for transfers between devices: 7.38 us -> 3.26 us  [exchange(): lax.all_to_all(values, axis, split_axis=0, concat_axis=0, axis_index_grou...]
    broadcast_in_dim x1, local copies, waits for them, and re-layouts: 1.31 us -> 0.71 us  [body(): jnp.broadcast_to(offsets.T[None], (bands,) + offsets.T.shape)]
  transfers between devices with their start and end apart: 2 -> 1, of which waited for: 2 -> 1; matrix products, arithmetic and copies ran while one was open for 0% -> 0% of each run, Pallas kernels for 5% -> 5%
where the time goes in v3:
time: 37.6 us; the launch traced here: 37.3 us
  blocking collectives  20.4 us (54%)
  Pallas kernels  5.96 us (16%)
  starting transfers between devices  3.98 us (11%)
  waiting for transfers between devices  3.26 us (9%)
  local copies, waits for them, and re-layouts  2.39 us (6%)
  between operations  0.69 us (2%)
  other arithmetic  0.61 us (2%)
    all_to_all x2, blocking collectives, exchange(): lax.all_to_all(values, axis, split_axis=0, concat_axis=0, axis_index_grou...  20.4 us
    all_to_all x1, starting transfers between devices, exchange(): lax.all_to_all(values, axis, split_axis=0, concat_axis=0, axis_index_grou...  3.98 us
    all_to_all x1, waiting for transfers between devices, exchange(): lax.all_to_all(values, axis, split_axis=0, concat_axis=0, axis_index_grou...  3.26 us
    pallas_call x1, Pallas kernels, pick(): pl.pallas_call(functools.partial(pick_kernel, bands_in, bands_out), out_s...  2.25 us
    pallas_call x1, Pallas kernels, prepare(): pl.pallas_call(functools.partial(prepare_kernel, first, run), out_shape=(...  1.92 us
    pallas_call x1, Pallas kernels, statistic(): pl.pallas_call(statistic_kernel, out_shape=(jax.ShapeDtypeStruct((count *...  1.78 us
    unnamed x10, local copies, waits for them, and re-layouts  1.61 us
  transfers between devices with their start and end apart: 1, of which 1 were waited for; matrix products, arithmetic and copies ran while one was open for 0% of the time, Pallas kernels for 5%

profile of v3, /device:TPU:0, one launch (start us, length us, event | category | flops | bytes accessed | tf_op | source)
XLA Modules:
  0.0 37.3 jit_solution(13224627410229205763)
XLA Ops:
  0.6 0.0 copy-start.3
  0.6 0.0 copy-start.4
  0.7 0.0 copy-start.1
  0.7 0.0 copy-start.2
  0.7 0.7 %broadcast_in_dim.6 = s32[8,2,256]{2,1,0:T(2,128)S(1)} broadcast(s32[2,256]{1,0:T(2,128)} %bitcast.9), dimensions={1,2} | broadcast | bytes 18432 | tf_op jit(solution)/shard_map/broadcast_in_dim | solution.py:257
  1.4 11.8 %all_to_all.15.offset_ref = s32[8,2,256]{2,1,0:T(2,128)S(1)} all-to-all(s32[8,2,256]{2,1,0:T(2,128)S(1)} %broadcast_in_dim.6), channel_id=1, replica_groups={{8,2,4,6,0,10,12,14},{9,3,5,7,1,11,13,15},{24,18,20,22,16,26,28,30},{25..., dimensions={0} | all-to-all | bytes 32768 | tf_op jit(solution)/shard_map/all_to_all | solution.py:246
  13.2 0.0 copy-start
  13.2 1.6 %copy-done = bf16[32,4,8192]{2,1,0:T(4,128)(2,1)S(1)} copy-done((bf16[32,4,8192]{2,1,0:T(4,128)(2,1)S(1)}, bf16[32,4,8192]{2,1,0:T(4,128)(2,1)}, u32[]{:S(2)}) %copy-start) | copy-done | bytes 2097176
  14.8 2.3 %pick.1 = bf16[512,128]{1,0:T(8,128)(2,1)} custom-call(s32[8,2,256]{2,1,0:T(2,128)S(1)} %all_to_all.15.offset_ref, bf16[32,4,8192]{2,1,0:T(4,128)(2,1)S(1)} %copy-done), custom_call_target="tpu_custom_call" | custom-call | flops 10000000 | bytes 2097152 | tf_op jit(solution)/shard_map/pick/pallas_call | solution.py:105
  17.1 4.0 %all-to-all-start.1 = ((bf16[16,32,128]{2,1,0:T(8,128)(2,1)}), bf16[16,32,128]{2,1,0:T(8,128)(2,1)S(1)}, u32[]{:S(2)}, u32[]{:S(2)}) async-start(bf16[16,32,128]{2,1,0:T(8,128)(2,1)} %bitcast.1), calls=%async_computation.1 | async-start | bytes 262144 | tf_op jit(solution)/shard_map/all_to_all | solution.py:246
  21.0 0.0 copy-done.4
  21.0 0.1 broadcast_in_dim.7.starts_ref
  21.1 0.0 copy-done.3
  21.1 0.0 copy-done.1
  21.1 0.0 copy-done.2
  21.1 1.9 %prepare.1 = (bf16[512,512]{1,0:T(8,128)(2,1)S(1)}, f32[2,512,128]{2,1,0:T(8,128)S(1)}, f32[3,512,128]{2,1,0:T(8,128)S(1)}, bf16[256,1024]{1,0:T(8,128)(2,1)S(1)}) custom-call(s32[32]{0:T(128)S(1)} %copy-done.3, s32[32,128]{1,0:T(8,128)S(1)} %broadcast_in_dim.7.starts_ref, f32[4,512]{1,0:T(4,128)S(1)} %bitcast.7, f32[1,256]{1,0:T(1,128)S(1)} %bitcast.8), custom_call_target="tpu_custom_call" | custom-call | flops 100000000 | bytes 4000000 | tf_op jit(solution)/shard_map/prepare/pallas_call | solution.py:183
  23.1 3.3 %all-to-all-done.1 = bf16[16,32,128]{2,1,0:T(8,128)(2,1)S(1)} async-done(((bf16[16,32,128]{2,1,0:T(8,128)(2,1)}), bf16[16,32,128]{2,1,0:T(8,128)(2,1)S(1)}, u32[]{:S(2)}, u32[]{:S(2)}) %all-to-all-start.1) | async-done | bytes 131104 | tf_op jit(solution)/shard_map/all_to_all | solution.py:246
  26.3 1.8 %statistic.1 = (f32[512,256]{1,0:T(8,128)}, f32[8,16,128]{2,1,0:T(8,128)S(1)}) custom-call(bf16[512,128]{1,0:T(8,128)(2,1)S(1)} %bitcast.6, bf16[512,512]{1,0:T(8,128)(2,1)S(1)} %get-tuple-element.18.mask_ref, f32[2,512,128]{2,1,0:T(8,128)S(1)} %get-tuple-element.19.weigh_ref, f32[3,512,128]{2,1,0:T(8,128)S(1)} %get-tuple-element.20.coef_ref, ...), custom_call_target="tpu_custom_call" | custom-call | flops 400000000 | bytes 4000000 | tf_op jit(solution)/shard_map/statistic/pallas_call | solution.py:230
  28.1 8.6 %all_to_all.16 = f32[8,16,128]{2,1,0:T(8,128)S(1)} all-to-all(f32[8,16,128]{2,1,0:T(8,128)S(1)} %get-tuple-element.23), channel_id=1, replica_groups={{8,2,4,6,0,10,12,14},{9,3,5,7,1,11,13,15},{24,18,20,22,16,26,28,30},{25..., dimensions={0} | all-to-all | bytes 131072 | tf_op jit(solution)/shard_map/all_to_all | solution.py:246
  36.7 0.6 %slice_reduce_fusion = f32[16,32]{1,0:T(8,128)} fusion(f32[8,16,128]{2,1,0:T(8,128)S(1)} %all_to_all.16), kind=kLoop, calls=%fused_computation | loop fusion | flops 3584 | bytes 18432 | tf_op jit(solution)/shard_map/reduce_max | solution.py:264
Async XLA Ops:
  0.6 20.5 %copy-start.3 = (s32[32]{0:T(128)S(1)}, s32[32]{0:T(128)}, u32[]{:S(2)}) copy-start(s32[32]{0:T(128)} %durations_ref) | copy-start | bytes 388
  0.6 20.4 %copy-start.4 = (s32[32]{0:T(128)S(1)}, s32[32]{0:T(128)}, u32[]{:S(2)}) copy-start(s32[32]{0:T(128)} %param.10) | copy-start | bytes 388
  0.7 20.5 %copy-start.1 = (f32[512,4]{0,1:T(4,128)S(1)}, f32[512,4]{0,1:T(4,128)}, u32[]{:S(2)}) copy-start(f32[512,4]{0,1:T(4,128)} %param.9) | copy-start | bytes 24580
  0.7 20.5 %copy-start.2 = (f32[256]{0:T(256)S(1)}, f32[256]{0:T(256)}, u32[]{:S(2)}) copy-start(f32[256]{0:T(256)} %param.8) | copy-start | bytes 3076
  13.2 1.6 %copy-start = (bf16[32,4,8192]{2,1,0:T(4,128)(2,1)S(1)}, bf16[32,4,8192]{2,1,0:T(4,128)(2,1)}, u32[]{:S(2)}) copy-start(bf16[32,4,8192]{2,1,0:T(4,128)(2,1)} %spec_ref.1) | copy-start | bytes 6291460
  17.1 9.3 %all-to-all-start.1 = ((bf16[16,32,128]{2,1,0:T(8,128)(2,1)}), bf16[16,32,128]{2,1,0:T(8,128)(2,1)S(1)}, u32[]{:S(2)}, u32[]{:S(2)}) async-start(bf16[16,32,128]{2,1,0:T(8,128)(2,1)} %bitcast.1), calls=%async_computation.1 | async-start | bytes 262144 | tf_op jit(solution)/shard_map/all_to_all | solution.py:246

commit v4 on v3

--- a/solution.py
+++ b/solution.py
@@ -20,6 +20,27 @@
     members = list(range(size))
     members[0], members[first] = first, 0
     return members
+
+
+def repeat_kernel(in_ref, out_ref, sems):
+    copies = [pltpu.make_async_copy(in_ref, out_ref.at[n], sems.at[n]) for n in range(out_ref.shape[0])]
+    for copy in copies:
+        copy.start()
+    for copy in copies:
+        copy.wait()
+
+
+def repeat(values, count):
+    return pl.pallas_call(
+        repeat_kernel,
+        out_shape=jax.ShapeDtypeStruct((count,) + values.shape, values.dtype),
+        in_specs=[pl.BlockSpec(memory_space=pl.ANY)],
+        out_specs=pl.BlockSpec(memory_space=pltpu.VMEM),
+        scratch_shapes=[pltpu.SemaphoreType.DMA((count,))],
+        compiler_params=pltpu.CompilerParams(vmem_limit_bytes=8 * 1024 * 1024),
+        cost_estimate=pl.CostEstimate(flops=0, bytes_accessed=32_000_000, transcendentals=0),
+        name="repeat",
+    )(values)
 
 
 def pick_kernel(bands_in, bands_out, offset_ref, spec_ref, out_ref, place_ref, turn_ref, tile_ref, sems):
@@ -254,7 +275,7 @@
     by_band = order(bands, bands // 2)
     first = (cores - 1) * bands + bands // 2
     by_run = order(cores * bands, first)
-    known = exchange(jnp.broadcast_to(offsets.T[None], (bands,) + offsets.T.shape), "tmpl", by_band)
+    known = exchange(repeat(offsets.T, bands), "tmpl", by_band)
     windows = pick(known, spectra, by_band, [run % bands for run in by_run])
     windows, *late = lax.optimization_barrier((windows, durations, starts, antenna, fractions))
     durations, starts, antenna, fractions = late

time: 37.6 us -> 37.7 us (level)
    broadcast_in_dim x1 -> x0, local copies, waits for them, and re-layouts: 0.71 us -> none  [body(): jnp.broadcast_to(offsets.T[None], (bands,) + offsets.T.shape)]
    unnamed x10 -> x12, local copies, waits for them, and re-layouts: 1.61 us -> 2.29 us
where the time goes in v4:
time: 37.7 us; the launch traced here: 37.4 us
  blocking collectives  20.4 us (54%)
  Pallas kernels  6.06 us (16%)
  starting transfers between devices  3.98 us (11%)
  waiting for transfers between devices  3.26 us (9%)
  local copies, waits for them, and re-layouts  2.36 us (6%)
  between operations  0.69 us (2%)
  other arithmetic  0.61 us (2%)
    all_to_all x2, blocking collectives, exchange(): lax.all_to_all(values, axis, split_axis=0, concat_axis=0, axis_index_grou...  20.4 us
    all_to_all x1, starting transfers between devices, exchange(): lax.all_to_all(values, axis, split_axis=0, concat_axis=0, axis_index_grou...  3.98 us
    all_to_all x1, waiting for transfers between devices, exchange(): lax.all_to_all(values, axis, split_axis=0, concat_axis=0, axis_index_grou...  3.26 us
    unnamed x12, local copies, waits for them, and re-layouts  2.29 us
    pallas_call x1, Pallas kernels, pick(): pl.pallas_call(functools.partial(pick_kernel, bands_in, bands_out), out_s...  2.25 us
    pallas_call x1, Pallas kernels, prepare(): pl.pallas_call(functools.partial(prepare_kernel, first, run), out_shape=(...  1.92 us
    pallas_call x1, Pallas kernels, statistic(): pl.pallas_call(statistic_kernel, out_shape=(jax.ShapeDtypeStruct((count *...  1.8 us
  transfers between devices with their start and end apart: 1, of which 1 were waited for; matrix products, arithmetic and copies ran while one was open for 0% of the time, Pallas kernels for 5%

profile of v4, /device:TPU:0, one launch (start us, length us, event | category | flops | bytes accessed | tf_op | source)
XLA Modules:
  0.0 37.4 jit_solution(4219058905915119493)
XLA Ops:
  0.6 0.0 copy-start.4
  0.6 0.0 copy-start.3
  0.7 0.0 copy-start.1
  0.7 0.7 %copy-done.1 = s32[256,2]{0,1:T(2,128)S(1)} copy-done((s32[256,2]{0,1:T(2,128)S(1)}, s32[256,2]{0,1:T(2,128)}, u32[]{:S(2)}) %copy-start.1) | copy-done | bytes 2072
  1.3 0.0 copy-start.5
  1.3 0.0 copy-start.2
  1.4 0.1 repeat.1
  1.5 11.8 %all_to_all.15.offset_ref = s32[8,2,256]{2,1,0:T(2,128)S(1)} all-to-all(s32[8,2,256]{2,1,0:T(2,128)S(1)} %repeat.1), channel_id=1, replica_groups={{8,2,4,6,0,10,12,14},{9,3,5,7,1,11,13,15},{24,18,20,22,16,26,28,30},{25..., dimensions={0} | all-to-all | bytes 32768 | tf_op jit(solution)/shard_map/all_to_all | solution.py:267
  13.3 0.0 copy-start
  13.3 1.6 %copy-done = bf16[32,4,8192]{2,1,0:T(4,128)(2,1)S(1)} copy-done((bf16[32,4,8192]{2,1,0:T(4,128)(2,1)S(1)}, bf16[32,4,8192]{2,1,0:T(4,128)(2,1)}, u32[]{:S(2)}) %copy-start) | copy-done | bytes 2097176
  14.9 2.3 %pick.1 = bf16[512,128]{1,0:T(8,128)(2,1)} custom-call(s32[8,2,256]{2,1,0:T(2,128)S(1)} %all_to_all.15.offset_ref, bf16[32,4,8192]{2,1,0:T(4,128)(2,1)S(1)} %copy-done), custom_call_target="tpu_custom_call" | custom-call | flops 10000000 | bytes 2097152 | tf_op jit(solution)/shard_map/pick/pallas_call | solution.py:126
  17.1 4.0 %all-to-all-start.1 = ((bf16[16,32,128]{2,1,0:T(8,128)(2,1)}), bf16[16,32,128]{2,1,0:T(8,128)(2,1)S(1)}, u32[]{:S(2)}, u32[]{:S(2)}) async-start(bf16[16,32,128]{2,1,0:T(8,128)(2,1)} %bitcast.1), calls=%async_computation.1 | async-start | bytes 262144 | tf_op jit(solution)/shard_map/all_to_all | solution.py:267
  21.1 0.0 copy-done.5
  21.1 0.1 broadcast_in_dim.4.starts_ref
  21.2 0.0 copy-done.4
  21.2 0.0 copy-done.3
  21.2 0.0 copy-done.2
  21.2 1.9 %prepare.1 = (bf16[512,512]{1,0:T(8,128)(2,1)S(1)}, f32[2,512,128]{2,1,0:T(8,128)S(1)}, f32[3,512,128]{2,1,0:T(8,128)S(1)}, bf16[256,1024]{1,0:T(8,128)(2,1)S(1)}) custom-call(s32[32]{0:T(128)S(1)} %copy-done.4, s32[32,128]{1,0:T(8,128)S(1)} %broadcast_in_dim.4.starts_ref, f32[4,512]{1,0:T(4,128)S(1)} %bitcast.8, f32[1,256]{1,0:T(1,128)S(1)} %bitcast.9), custom_call_target="tpu_custom_call" | custom-call | flops 100000000 | bytes 4000000 | tf_op jit(solution)/shard_map/prepare/pallas_call | solution.py:204
  23.1 3.3 %all-to-all-done.1 = bf16[16,32,128]{2,1,0:T(8,128)(2,1)S(1)} async-done(((bf16[16,32,128]{2,1,0:T(8,128)(2,1)}), bf16[16,32,128]{2,1,0:T(8,128)(2,1)S(1)}, u32[]{:S(2)}, u32[]{:S(2)}) %all-to-all-start.1) | async-done | bytes 131104 | tf_op jit(solution)/shard_map/all_to_all | solution.py:267
  26.4 1.8 %statistic.1 = (f32[512,256]{1,0:T(8,128)}, f32[8,16,128]{2,1,0:T(8,128)S(1)}) custom-call(bf16[512,128]{1,0:T(8,128)(2,1)S(1)} %bitcast.6, bf16[512,512]{1,0:T(8,128)(2,1)S(1)} %get-tuple-element.18.mask_ref, f32[2,512,128]{2,1,0:T(8,128)S(1)} %get-tuple-element.19.weigh_ref, f32[3,512,128]{2,1,0:T(8,128)S(1)} %get-tuple-element.20.coef_ref, ...), custom_call_target="tpu_custom_call" | custom-call | flops 400000000 | bytes 4000000 | tf_op jit(solution)/shard_map/statistic/pallas_call | solution.py:251
  28.2 8.6 %all_to_all.16 = f32[8,16,128]{2,1,0:T(8,128)S(1)} all-to-all(f32[8,16,128]{2,1,0:T(8,128)S(1)} %get-tuple-element.23), channel_id=1, replica_groups={{8,2,4,6,0,10,12,14},{9,3,5,7,1,11,13,15},{24,18,20,22,16,26,28,30},{25..., dimensions={0} | all-to-all | bytes 131072 | tf_op jit(solution)/shard_map/all_to_all | solution.py:267
  36.8 0.6 %slice_reduce_fusion = f32[16,32]{1,0:T(8,128)} fusion(f32[8,16,128]{2,1,0:T(8,128)S(1)} %all_to_all.16), kind=kLoop, calls=%fused_computation | loop fusion | flops 3584 | bytes 18432 | tf_op jit(solution)/shard_map/reduce_max | solution.py:285
Async XLA Ops:
  0.6 20.6 %copy-start.4 = (s32[32]{0:T(128)S(1)}, s32[32]{0:T(128)}, u32[]{:S(2)}) copy-start(s32[32]{0:T(128)} %durations_ref) | copy-start | bytes 388
  0.6 20.6 %copy-start.3 = (f32[256]{0:T(256)S(1)}, f32[256]{0:T(256)}, u32[]{:S(2)}) copy-start(f32[256]{0:T(256)} %param.8) | copy-start | bytes 3076
  0.7 0.7 %copy-start.1 = (s32[256,2]{0,1:T(2,128)S(1)}, s32[256,2]{0,1:T(2,128)}, u32[]{:S(2)}) copy-start(s32[256,2]{0,1:T(2,128)} %param.7) | copy-start | bytes 6148
  1.3 19.8 %copy-start.5 = (s32[32]{0:T(128)S(1)}, s32[32]{0:T(128)}, u32[]{:S(2)}) copy-start(s32[32]{0:T(128)} %param.10) | copy-start | bytes 388
  1.3 19.9 %copy-start.2 = (f32[512,4]{0,1:T(4,128)S(1)}, f32[512,4]{0,1:T(4,128)}, u32[]{:S(2)}) copy-start(f32[512,4]{0,1:T(4,128)} %param.9) | copy-start | bytes 24580
  13.3 1.6 %copy-start = (bf16[32,4,8192]{2,1,0:T(4,128)(2,1)S(1)}, bf16[32,4,8192]{2,1,0:T(4,128)(2,1)}, u32[]{:S(2)}) copy-start(bf16[32,4,8192]{2,1,0:T(4,128)(2,1)} %spec_ref.1) | copy-start | bytes 6291460
  17.1 9.3 %all-to-all-start.1 = ((bf16[16,32,128]{2,1,0:T(8,128)(2,1)}), bf16[16,32,128]{2,1,0:T(8,128)(2,1)S(1)}, u32[]{:S(2)}, u32[]{:S(2)}) async-start(bf16[16,32,128]{2,1,0:T(8,128)(2,1)} %bitcast.1), calls=%async_computation.1 | async-start | bytes 262144 | tf_op jit(solution)/shard_map/all_to_all | solution.py:267

commit v5 on v3

--- a/solution.py
+++ b/solution.py
@@ -22,13 +22,18 @@
     return members
 
 
-def pick_kernel(bands_in, bands_out, offset_ref, spec_ref, out_ref, place_ref, turn_ref, tile_ref, sems):
+def pick_kernel(bands_in, bands_out, offset_ref, spec_ref, out_ref, held_ref, place_ref, turn_ref, tile_ref, in_sems, sems):
     rows, _, bins = spec_ref.shape
     bands, blocks, _ = offset_ref.shape
     band_width = bins // bands
     groups = rows // 8
     chunks = band_width // LANES
     width = blocks * W
+    arrivals = []
+    for band in range(bands):
+        columns = pl.ds(band * band_width, band_width)
+        arrivals.append(pltpu.make_async_copy(spec_ref.at[:, :, columns], held_ref.at[:, :, columns], in_sems.at[band]))
+        arrivals[-1].start()
     first = lax.axis_index("tmpl").astype(jnp.int32) * rows
     columns = pl.ds(pl.multiple_of(first // LANES * LANES, LANES), LANES)
     offsets = jnp.concatenate([offset_ref[bands_in.index(band), :, columns] for band in range(bands)], axis=0).astype(jnp.float32)
@@ -58,7 +63,7 @@
             for group in range(groups):
                 for chunk in range(chunks):
                     columns = pl.ds(band * band_width + chunk * LANES, LANES)
-                    values = spec_ref[pl.ds(group * 8 + pair * 2, 2), :, columns]
+                    values = held_ref[pl.ds(group * 8 + pair * 2, 2), :, columns]
                     values = values.astype(jnp.float32).reshape(8, LANES)
                     moved = jnp.take_along_axis(values, lane_id, axis=1, mode="promise_in_bounds")
                     tile = jnp.where(chosen == group * chunks + chunk, moved, tile)
@@ -78,6 +83,7 @@
 
     tiles, copies = {}, []
     for band in range(bands):
+        arrivals[band].wait()
         gather(band)
         tiles[band] = turn(band)
         if rows % 16 == 0:
@@ -105,15 +111,17 @@
     return pl.pallas_call(
         functools.partial(pick_kernel, bands_in, bands_out),
         out_shape=jax.ShapeDtypeStruct((out_rows, LANES), jnp.bfloat16),
-        in_specs=[vmem, vmem],
+        in_specs=[vmem, pl.BlockSpec(memory_space=pl.ANY)],
         out_specs=pl.BlockSpec(memory_space=pl.ANY),
         scratch_shapes=[
+            pltpu.VMEM(spectra.shape, spectra.dtype),
             pltpu.VMEM((bands, 4, 8, LANES), jnp.int32),
             pltpu.VMEM((bands, 32, LANES), jnp.float32),
             pltpu.VMEM((out_rows, LANES), jnp.bfloat16),
+            pltpu.SemaphoreType.DMA((bands,)),
             pltpu.SemaphoreType.DMA((len(bands_out),)),
         ],
-        compiler_params=pltpu.CompilerParams(vmem_limit_bytes=8 * 1024 * 1024),
+        compiler_params=pltpu.CompilerParams(vmem_limit_bytes=52 * 1024 * 1024),
         cost_estimate=pl.CostEstimate(flops=10_000_000, bytes_accessed=2 * spectra.size, transcendentals=0),
         name="pick",
     )(offsets, spectra)

time: 37.6 us -> 37.4 us (level)
  local copies, waits for them, and re-layouts: 2.39 us -> 0.8 us
  Pallas kernels: 5.96 us -> 7.36 us
    unnamed x10 -> x8, local copies, waits for them, and re-layouts: 1.61 us -> 0.02 us
    pallas_call x1, Pallas kernels: 2.25 us -> 3.65 us  [pick(): pl.pallas_call(functools.partial(pick_kernel, bands_in, bands_out), out_s...]
where the time goes in v5:
time: 37.4 us; the launch traced here: 37.1 us
  blocking collectives  20.4 us (55%)
  Pallas kernels  7.36 us (20%)
  starting transfers between devices  3.98 us (11%)
  waiting for transfers between devices  3.26 us (9%)
  local copies, waits for them, and re-layouts  0.8 us (2%)
  between operations  0.69 us (2%)
  other arithmetic  0.61 us (2%)
    all_to_all x2, blocking collectives, exchange(): lax.all_to_all(values, axis, split_axis=0, concat_axis=0, axis_index_grou...  20.4 us
    all_to_all x1, starting transfers between devices, exchange(): lax.all_to_all(values, axis, split_axis=0, concat_axis=0, axis_index_grou...  3.98 us
    pallas_call x1, Pallas kernels, pick(): pl.pallas_call(functools.partial(pick_kernel, bands_in, bands_out), out_s...  3.65 us
    all_to_all x1, waiting for transfers between devices, exchange(): lax.all_to_all(values, axis, split_axis=0, concat_axis=0, axis_index_grou...  3.26 us
    pallas_call x1, Pallas kernels, prepare(): pl.pallas_call(functools.partial(prepare_kernel, first, run), out_shape=(...  1.92 us
    pallas_call x1, Pallas kernels, statistic(): pl.pallas_call(statistic_kernel, out_shape=(jax.ShapeDtypeStruct((count *...  1.79 us
  transfers between devices with their start and end apart: 1, of which 1 were waited for; matrix products, arithmetic and copies ran while one was open for 0% of the time, Pallas kernels for 5%

profile of v5, /device:TPU:0, one launch (start us, length us, event | category | flops | bytes accessed | tf_op | source)
XLA Modules:
  0.0 37.1 jit_solution(8033267671795439204)
XLA Ops:
  0.6 0.0 copy-start.2
  0.6 0.0 copy-start.3
  0.7 0.0 copy-start
  0.7 0.0 copy-start.1
  0.7 0.7 %broadcast_in_dim.6 = s32[8,2,256]{2,1,0:T(2,128)S(1)} broadcast(s32[2,256]{1,0:T(2,128)} %bitcast.9), dimensions={1,2} | broadcast | bytes 18432 | tf_op jit(solution)/shard_map/broadcast_in_dim | solution.py:265
  1.4 11.8 %all_to_all.15.offset_ref = s32[8,2,256]{2,1,0:T(2,128)S(1)} all-to-all(s32[8,2,256]{2,1,0:T(2,128)S(1)} %broadcast_in_dim.6), channel_id=1, replica_groups={{8,2,4,6,0,10,12,14},{9,3,5,7,1,11,13,15},{24,18,20,22,16,26,28,30},{25..., dimensions={0} | all-to-all | bytes 32768 | tf_op jit(solution)/shard_map/all_to_all | solution.py:254
  13.2 3.7 %pick.1 = bf16[512,128]{1,0:T(8,128)(2,1)} custom-call(s32[8,2,256]{2,1,0:T(2,128)S(1)} %all_to_all.15.offset_ref, bf16[32,4,8192]{2,1,0:T(4,128)(2,1)} %spec_ref.1), custom_call_target="tpu_custom_call" | custom-call | flops 10000000 | bytes 2097152 | tf_op jit(solution)/shard_map/pick/pallas_call | solution.py:111
  16.9 4.0 %all-to-all-start.1 = ((bf16[16,32,128]{2,1,0:T(8,128)(2,1)}), bf16[16,32,128]{2,1,0:T(8,128)(2,1)S(1)}, u32[]{:S(2)}, u32[]{:S(2)}) async-start(bf16[16,32,128]{2,1,0:T(8,128)(2,1)} %bitcast.1), calls=%async_computation.1 | async-start | bytes 262144 | tf_op jit(solution)/shard_map/all_to_all | solution.py:254
  20.8 0.0 copy-done.3
  20.9 0.1 broadcast_in_dim.7.starts_ref
  20.9 0.0 copy-done.2
  20.9 0.0 copy-done
  20.9 0.0 copy-done.1
  20.9 1.9 %prepare.1 = (bf16[512,512]{1,0:T(8,128)(2,1)S(1)}, f32[2,512,128]{2,1,0:T(8,128)S(1)}, f32[3,512,128]{2,1,0:T(8,128)S(1)}, bf16[256,1024]{1,0:T(8,128)(2,1)S(1)}) custom-call(s32[32]{0:T(128)S(1)} %copy-done.2, s32[32,128]{1,0:T(8,128)S(1)} %broadcast_in_dim.7.starts_ref, f32[4,512]{1,0:T(4,128)S(1)} %bitcast.7, f32[1,256]{1,0:T(1,128)S(1)} %bitcast.8), custom_call_target="tpu_custom_call" | custom-call | flops 100000000 | bytes 4000000 | tf_op jit(solution)/shard_map/prepare/pallas_call | solution.py:191
  22.9 3.3 %all-to-all-done.1 = bf16[16,32,128]{2,1,0:T(8,128)(2,1)S(1)} async-done(((bf16[16,32,128]{2,1,0:T(8,128)(2,1)}), bf16[16,32,128]{2,1,0:T(8,128)(2,1)S(1)}, u32[]{:S(2)}, u32[]{:S(2)}) %all-to-all-start.1) | async-done | bytes 131104 | tf_op jit(solution)/shard_map/all_to_all | solution.py:254
  26.1 1.8 %statistic.1 = (f32[512,256]{1,0:T(8,128)}, f32[8,16,128]{2,1,0:T(8,128)S(1)}) custom-call(bf16[512,128]{1,0:T(8,128)(2,1)S(1)} %bitcast.6, bf16[512,512]{1,0:T(8,128)(2,1)S(1)} %get-tuple-element.18.mask_ref, f32[2,512,128]{2,1,0:T(8,128)S(1)} %get-tuple-element.19.weigh_ref, f32[3,512,128]{2,1,0:T(8,128)S(1)} %get-tuple-element.20.coef_ref, ...), custom_call_target="tpu_custom_call" | custom-call | flops 400000000 | bytes 4000000 | tf_op jit(solution)/shard_map/statistic/pallas_call | solution.py:238
  27.9 8.6 %all_to_all.16 = f32[8,16,128]{2,1,0:T(8,128)S(1)} all-to-all(f32[8,16,128]{2,1,0:T(8,128)S(1)} %get-tuple-element.23), channel_id=1, replica_groups={{8,2,4,6,0,10,12,14},{9,3,5,7,1,11,13,15},{24,18,20,22,16,26,28,30},{25..., dimensions={0} | all-to-all | bytes 131072 | tf_op jit(solution)/shard_map/all_to_all | solution.py:254
  36.5 0.6 %slice_reduce_fusion = f32[16,32]{1,0:T(8,128)} fusion(f32[8,16,128]{2,1,0:T(8,128)S(1)} %all_to_all.16), kind=kLoop, calls=%fused_computation | loop fusion | flops 3584 | bytes 18432 | tf_op jit(solution)/shard_map/reduce_max | solution.py:272
Async XLA Ops:
  0.6 20.3 %copy-start.2 = (s32[32]{0:T(128)S(1)}, s32[32]{0:T(128)}, u32[]{:S(2)}) copy-start(s32[32]{0:T(128)} %durations_ref) | copy-start | bytes 388
  0.6 20.2 %copy-start.3 = (s32[32]{0:T(128)S(1)}, s32[32]{0:T(128)}, u32[]{:S(2)}) copy-start(s32[32]{0:T(128)} %param.10) | copy-start | bytes 388
  0.7 20.3 %copy-start = (f32[512,4]{0,1:T(4,128)S(1)}, f32[512,4]{0,1:T(4,128)}, u32[]{:S(2)}) copy-start(f32[512,4]{0,1:T(4,128)} %param.9) | copy-start | bytes 24580
  0.7 20.3 %copy-start.1 = (f32[256]{0:T(256)S(1)}, f32[256]{0:T(256)}, u32[]{:S(2)}) copy-start(f32[256]{0:T(256)} %param.8) | copy-start | bytes 3076
  16.9 9.3 %all-to-all-start.1 = ((bf16[16,32,128]{2,1,0:T(8,128)(2,1)}), bf16[16,32,128]{2,1,0:T(8,128)(2,1)S(1)}, u32[]{:S(2)}, u32[]{:S(2)}) async-start(bf16[16,32,128]{2,1,0:T(8,128)(2,1)} %bitcast.1), calls=%async_computation.1 | async-start | bytes 262144 | tf_op jit(solution)/shard_map/all_to_all | solution.py:254

commit v6 on v3

--- a/solution.py
+++ b/solution.py
@@ -20,6 +20,25 @@
     members = list(range(size))
     members[0], members[first] = first, 0
     return members
+
+
+def hold_kernel(spec_ref, out_ref, sem):
+    copy = pltpu.make_async_copy(spec_ref, out_ref, sem)
+    copy.start()
+    copy.wait()
+
+
+def hold(spectra):
+    return pl.pallas_call(
+        hold_kernel,
+        out_shape=jax.ShapeDtypeStruct(spectra.shape, spectra.dtype),
+        in_specs=[pl.BlockSpec(memory_space=pl.ANY)],
+        out_specs=pl.BlockSpec(memory_space=pltpu.VMEM),
+        scratch_shapes=[pltpu.SemaphoreType.DMA],
+        compiler_params=pltpu.CompilerParams(vmem_limit_bytes=8 * 1024 * 1024),
+        cost_estimate=pl.CostEstimate(flops=0, bytes_accessed=4 * spectra.size, transcendentals=0),
+        name="hold",
+    )(spectra)
 
 
 def pick_kernel(bands_in, bands_out, offset_ref, spec_ref, out_ref, place_ref, turn_ref, tile_ref, sems):
@@ -255,7 +274,7 @@
     first = (cores - 1) * bands + bands // 2
     by_run = order(cores * bands, first)
     known = exchange(jnp.broadcast_to(offsets.T[None], (bands,) + offsets.T.shape), "tmpl", by_band)
-    windows = pick(known, spectra, by_band, [run % bands for run in by_run])
+    windows = pick(known, hold(spectra), by_band, [run % bands for run in by_run])
     windows, *late = lax.optimization_barrier((windows, durations, starts, antenna, fractions))
     durations, starts, antenna, fractions = late
     prepared = prepare(durations, starts, antenna, fractions, first, sft_rows, cores)

time: 37.6 us -> 36.8 us (0.979)
  blocking collectives: 20.4 us -> 8.59 us
  starting transfers between devices: 3.98 us -> 11.8 us
  waiting for transfers between devices: 3.26 us -> 5.66 us
  local copies, waits for them, and re-layouts: 2.39 us -> 2.98 us
    all_to_all x2 -> x1, blocking collectives: 20.4 us -> 8.59 us  [exchange(): lax.all_to_all(values, axis, split_axis=0, concat_axis=0, axis_index_grou...]
    all_to_all x1 -> x2, starting transfers between devices: 3.98 us -> 11.8 us  [exchange(): lax.all_to_all(values, axis, split_axis=0, concat_axis=0, axis_index_grou...]
    all_to_all x1 -> x2, waiting for transfers between devices: 3.26 us -> 5.66 us  [exchange(): lax.all_to_all(values, axis, split_axis=0, concat_axis=0, axis_index_grou...]
    broadcast_in_dim x1, local copies, waits for them, and re-layouts: 0.71 us -> 1.29 us  [body(): jnp.broadcast_to(offsets.T[None], (bands,) + offsets.T.shape)]
  transfers between devices with their start and end apart: 1 -> 2, of which waited for: 1 -> 2; matrix products, arithmetic and copies ran while one was open for 0% -> 0% of each run, Pallas kernels for 5% -> 6%
where the time goes in v6:
time: 36.8 us; the launch traced here: 36.5 us
  starting transfers between devices  11.8 us (32%)
  blocking collectives  8.59 us (23%)
  Pallas kernels  6.11 us (17%)
  waiting for transfers between devices  5.66 us (15%)
  local copies, waits for them, and re-layouts  2.98 us (8%)
  between operations  0.7 us (2%)
  other arithmetic  0.61 us (2%)
    all_to_all x2, starting transfers between devices, exchange(): lax.all_to_all(values, axis, split_axis=0, concat_axis=0, axis_index_grou...  11.8 us
    all_to_all x1, blocking collectives, exchange(): lax.all_to_all(values, axis, split_axis=0, concat_axis=0, axis_index_grou...  8.59 us
    all_to_all x2, waiting for transfers between devices, exchange(): lax.all_to_all(values, axis, split_axis=0, concat_axis=0, axis_index_grou...  5.66 us
    pallas_call x1, Pallas kernels, pick(): pl.pallas_call(functools.partial(pick_kernel, bands_in, bands_out), out_s...  2.25 us
    pallas_call x1, Pallas kernels, prepare(): pl.pallas_call(functools.partial(prepare_kernel, first, run), out_shape=(...  1.92 us
    pallas_call x1, Pallas kernels, statistic(): pl.pallas_call(statistic_kernel, out_shape=(jax.ShapeDtypeStruct((count *...  1.78 us
    unnamed x10, local copies, waits for them, and re-layouts  1.62 us
    broadcast_in_dim x1, local copies, waits for them, and re-layouts, body(): jnp.broadcast_to(offsets.T[None], (bands,) + offsets.T.shape)  1.29 us
  transfers between devices with their start and end apart: 2, of which 2 were waited for; matrix products, arithmetic and copies ran while one was open for 0% of the time, Pallas kernels for 6%

profile of v6, /device:TPU:0, one launch (start us, length us, event | category | flops | bytes accessed | tf_op | source)
XLA Modules:
  0.0 36.5 jit_solution(7424817900532842516)
XLA Ops:
  0.6 1.3 %broadcast_in_dim.6 = s32[8,2,256]{2,1,0:T(2,128)} broadcast(s32[2,256]{1,0:T(2,128)} %bitcast.9), dimensions={1,2} | broadcast | bytes 18432 | tf_op jit(solution)/shard_map/broadcast_in_dim | solution.py:276
  1.9 7.8 %all-to-all-start = ((s32[8,2,256]{2,1,0:T(2,128)}), s32[8,2,256]{2,1,0:T(2,128)S(1)}, u32[]{:S(2)}, u32[]{:S(2)}) async-start(s32[8,2,256]{2,1,0:T(2,128)} %broadcast_in_dim.6), calls=%async_computation | async-start | bytes 32768 | tf_op jit(solution)/shard_map/all_to_all | solution.py:265
  9.8 0.0 copy-start
  9.8 1.6 %copy-done = bf16[32,4,8192]{2,1,0:T(4,128)(2,1)S(1)} copy-done((bf16[32,4,8192]{2,1,0:T(4,128)(2,1)S(1)}, bf16[32,4,8192]{2,1,0:T(4,128)(2,1)}, u32[]{:S(2)}) %copy-start) | copy-done | bytes 2097176
  11.4 0.1 hold.1.spec_ref
  11.5 0.0 copy-start.4
  11.5 0.0 copy-start.1
  11.5 0.0 copy-start.2
  11.5 0.0 copy-start.3
  11.6 2.4 %all-to-all-done.offset_ref = s32[8,2,256]{2,1,0:T(2,128)S(1)} async-done(((s32[8,2,256]{2,1,0:T(2,128)}), s32[8,2,256]{2,1,0:T(2,128)S(1)}, u32[]{:S(2)}, u32[]{:S(2)}) %all-to-all-start) | async-done | bytes 16416 | tf_op jit(solution)/shard_map/all_to_all | solution.py:265
  14.0 2.3 %pick.1 = bf16[512,128]{1,0:T(8,128)(2,1)} custom-call(s32[8,2,256]{2,1,0:T(2,128)S(1)} %all-to-all-done.offset_ref, bf16[32,4,8192]{2,1,0:T(4,128)(2,1)S(1)} %hold.1.spec_ref), custom_call_target="tpu_custom_call" | custom-call | flops 10000000 | bytes 2097152 | tf_op jit(solution)/shard_map/pick/pallas_call | solution.py:124
  16.2 4.0 %all-to-all-start.1 = ((bf16[16,32,128]{2,1,0:T(8,128)(2,1)}), bf16[16,32,128]{2,1,0:T(8,128)(2,1)S(1)}, u32[]{:S(2)}, u32[]{:S(2)}) async-start(bf16[16,32,128]{2,1,0:T(8,128)(2,1)} %bitcast.1), calls=%async_computation.1 | async-start | bytes 262144 | tf_op jit(solution)/shard_map/all_to_all | solution.py:265
  20.2 0.0 copy-done.4
  20.2 0.1 broadcast_in_dim.7.starts_ref
  20.3 0.0 copy-done.1
  20.3 0.0 copy-done.2
  20.3 0.0 copy-done.3
  20.3 1.9 %prepare.1 = (bf16[512,512]{1,0:T(8,128)(2,1)S(1)}, f32[2,512,128]{2,1,0:T(8,128)S(1)}, f32[3,512,128]{2,1,0:T(8,128)S(1)}, bf16[256,1024]{1,0:T(8,128)(2,1)S(1)}) custom-call(s32[32]{0:T(128)S(1)} %copy-done.3, s32[32,128]{1,0:T(8,128)S(1)} %broadcast_in_dim.7.starts_ref, f32[4,512]{1,0:T(4,128)S(1)} %bitcast.7, f32[1,256]{1,0:T(1,128)S(1)} %bitcast.8), custom_call_target="tpu_custom_call" | custom-call | flops 100000000 | bytes 4000000 | tf_op jit(solution)/shard_map/prepare/pallas_call | solution.py:202
  22.2 3.3 %all-to-all-done.1 = bf16[16,32,128]{2,1,0:T(8,128)(2,1)S(1)} async-done(((bf16[16,32,128]{2,1,0:T(8,128)(2,1)}), bf16[16,32,128]{2,1,0:T(8,128)(2,1)S(1)}, u32[]{:S(2)}, u32[]{:S(2)}) %all-to-all-start.1) | async-done | bytes 131104 | tf_op jit(solution)/shard_map/all_to_all | solution.py:265
  25.5 1.8 %statistic.1 = (f32[512,256]{1,0:T(8,128)}, f32[8,16,128]{2,1,0:T(8,128)S(1)}) custom-call(bf16[512,128]{1,0:T(8,128)(2,1)S(1)} %bitcast.6, bf16[512,512]{1,0:T(8,128)(2,1)S(1)} %get-tuple-element.18.mask_ref, f32[2,512,128]{2,1,0:T(8,128)S(1)} %get-tuple-element.19.weigh_ref, f32[3,512,128]{2,1,0:T(8,128)S(1)} %get-tuple-element.20.coef_ref, ...), custom_call_target="tpu_custom_call" | custom-call | flops 400000000 | bytes 4000000 | tf_op jit(solution)/shard_map/statistic/pallas_call | solution.py:249
  27.3 8.6 %all_to_all.15 = f32[8,16,128]{2,1,0:T(8,128)S(1)} all-to-all(f32[8,16,128]{2,1,0:T(8,128)S(1)} %get-tuple-element.23), channel_id=1, replica_groups={{8,2,4,6,0,10,12,14},{9,3,5,7,1,11,13,15},{24,18,20,22,16,26,28,30},{25..., dimensions={0} | all-to-all | bytes 131072 | tf_op jit(solution)/shard_map/all_to_all | solution.py:265
  35.9 0.6 %slice_reduce_fusion = f32[16,32]{1,0:T(8,128)} fusion(f32[8,16,128]{2,1,0:T(8,128)S(1)} %all_to_all.15), kind=kLoop, calls=%fused_computation | loop fusion | flops 3584 | bytes 18432 | tf_op jit(solution)/shard_map/reduce_max | solution.py:283
Async XLA Ops:
  1.9 12.0 %all-to-all-start = ((s32[8,2,256]{2,1,0:T(2,128)}), s32[8,2,256]{2,1,0:T(2,128)S(1)}, u32[]{:S(2)}, u32[]{:S(2)}) async-start(s32[8,2,256]{2,1,0:T(2,128)} %broadcast_in_dim.6), calls=%async_computation | async-start | bytes 32768 | tf_op jit(solution)/shard_map/all_to_all | solution.py:265
  9.8 1.6 %copy-start = (bf16[32,4,8192]{2,1,0:T(4,128)(2,1)S(1)}, bf16[32,4,8192]{2,1,0:T(4,128)(2,1)}, u32[]{:S(2)}) copy-start(bf16[32,4,8192]{2,1,0:T(4,128)(2,1)} %spec_ref.1) | copy-start | bytes 6291460
  11.5 8.7 %copy-start.4 = (s32[32]{0:T(128)S(1)}, s32[32]{0:T(128)}, u32[]{:S(2)}) copy-start(s32[32]{0:T(128)} %param.10) | copy-start | bytes 388
  11.5 8.8 %copy-start.1 = (f32[512,4]{0,1:T(4,128)S(1)}, f32[512,4]{0,1:T(4,128)}, u32[]{:S(2)}) copy-start(f32[512,4]{0,1:T(4,128)} %param.9) | copy-start | bytes 24580
  11.5 8.7 %copy-start.2 = (f32[256]{0:T(256)S(1)}, f32[256]{0:T(256)}, u32[]{:S(2)}) copy-start(f32[256]{0:T(256)} %param.8) | copy-start | bytes 3076
  11.5 8.7 %copy-start.3 = (s32[32]{0:T(128)S(1)}, s32[32]{0:T(128)}, u32[]{:S(2)}) copy-start(s32[32]{0:T(128)} %durations_ref) | copy-start | bytes 388
  16.2 9.3 %all-to-all-start.1 = ((bf16[16,32,128]{2,1,0:T(8,128)(2,1)}), bf16[16,32,128]{2,1,0:T(8,128)(2,1)S(1)}, u32[]{:S(2)}, u32[]{:S(2)}) async-start(bf16[16,32,128]{2,1,0:T(8,128)(2,1)} %bitcast.1), calls=%async_computation.1 | async-start | bytes 262144 | tf_op jit(solution)/shard_map/all_to_all | solution.py:265
